TPU v7x, 512 devices: a whole 4x8x8 slice. The times are simulated.
512 devices in a mesh: prompt: 64 (over y, z), seq: 8 (over x, core).
Axes of the slice: x: 4, y: 8, z: 8, core: 2. Of those that a mesh axis runs over, the one named last changes fastest.
Arguments:
- beam_rows: bfloat16 [2, 4096, 5120], P(None, 'prompt', 'seq'), may hold values from -240 to 240
- route: int32 [2, 4096, 1], P(None, 'prompt'), may hold values from 0 to 63; in each aligned block of 64 rows (0 to 63, 64 to 127, ..., all dimensions but the last counted through in order) at most 2 rows name the same one
- parent: int32 [2, 4096], P(None, 'prompt'), may hold values from 0 to 31
- prefix_kv: bfloat16 [64, 1024, 1024], P('prompt', 'seq'), may hold values from -6 to 6
- pages: bfloat16 [2048, 128, 1024], P('prompt', 'seq'), may hold values from -6 to 6
Outputs:
- attended: bfloat16 [2, 4096, 4096], P(None, 'prompt', 'seq')
Inputs may be any that keep to these rules, and one draw needn't show every extreme that they name: `route`: in each step, among the 64 rows of one device along prompt at most 2 name the same prompt. `parent`: index of a page among the 32 pages held by the same index of prompt as the row.
All inputs are finite; a program needn't handle non-finite values.
Results may differ from a plain program's by a relative error of at most 0.0042.
Values may be sent and summed in bfloat16 or wider, within the bound.
No kernel may reach another device: no remote copies, remote signals or barrier semaphores. Data moves between devices by JAX's collectives and lax.ppermute only.
A program may use at most 128 MiB of HBM per device.

v0:
```python
import jax
import jax.numpy as jnp
from jax import lax
from jax.sharding import PartitionSpec as P

HQ = 32
KVH = 4
DH = 128


def whole_rows(pieces):
    return lax.all_gather(pieces, "seq", axis=1, tiled=True)


def slot_positions(route_column, slot_cap, prompt_count):
    targets = jnp.arange(prompt_count, dtype=jnp.int32)
    onehot = (route_column[:, None] == targets[None, :]).astype(jnp.int32)
    ranking = jnp.sum(jnp.cumsum(onehot, axis=0) * onehot, axis=1) - 1
    return route_column * slot_cap + ranking


def spread(values, position, slot_total, prompt_count):
    empty = jnp.zeros((slot_total,) + values.shape[1:], values.dtype)
    filled = empty.at[position].set(values)
    return filled.reshape((prompt_count, slot_total // prompt_count) + values.shape[1:])


def split_kv(block_rows):
    key_rows = block_rows[..., : KVH * DH].reshape(block_rows.shape[:-1] + (KVH, DH))
    value_rows = block_rows[..., KVH * DH :].reshape(block_rows.shape[:-1] + (KVH, DH))
    return (key_rows, value_rows)


def finish_stats(scores):
    highest = jnp.max(scores, axis=-1)
    weights = jnp.exp(scores - highest[..., None]).astype(jnp.bfloat16)
    totals = jnp.sum(weights, axis=-1, dtype=jnp.float32)
    return (highest, totals, weights)


def shared_partial(query_flat, block_rows):
    queries = query_flat.reshape(query_flat.shape[0], KVH, HQ // KVH, DH)
    key_rows, value_rows = split_kv(block_rows)
    scores = jnp.einsum(
        "skgd,tkd->skgt", queries, key_rows, preferred_element_type=jnp.float32
    ) * DH ** (-0.5)
    highest, totals, weights = finish_stats(scores)
    weighted = jnp.einsum("skgt,tkd->skgd", weights, value_rows, preferred_element_type=jnp.float32)
    return (highest, totals, weighted)


def page_partial(query_flat, page_rows):
    queries = query_flat.reshape(query_flat.shape[0], KVH, HQ // KVH, DH)
    key_rows, value_rows = split_kv(page_rows)
    scores = jnp.einsum(
        "skgd,stkd->skgt", queries, key_rows, preferred_element_type=jnp.float32
    ) * DH ** (-0.5)
    highest, totals, weights = finish_stats(scores)
    weighted = jnp.einsum(
        "skgt,stkd->skgd", weights, value_rows, preferred_element_type=jnp.float32
    )
    return (highest, totals, weighted)


def join_parts(first, second):
    highest = jnp.maximum(first[0], second[0])
    factor_one = jnp.exp(first[0] - highest)
    factor_two = jnp.exp(second[0] - highest)
    totals = first[1] * factor_one + second[1] * factor_two
    weighted = first[2] * factor_one[..., None] + second[2] * factor_two[..., None]
    return (highest, totals, weighted)


def combine_seq(parts):
    highest = lax.pmax(parts[0], "seq")
    factor = jnp.exp(parts[0] - highest)
    totals = lax.psum(parts[1] * factor, "seq")
    scaled = (parts[2] * factor[..., None]).reshape(parts[2].shape[0], HQ * DH)
    shares = lax.psum_scatter(scaled, "seq", scatter_dimension=1, tiled=True)
    return (highest, totals, shares)


def finish_rows(combined, row_values, seq_count):
    highest, totals, shares = combined
    row_count = row_values.shape[0]
    head_part = HQ // seq_count
    first_head = lax.axis_index("seq") * head_part
    high_heads = lax.dynamic_slice_in_dim(highest.reshape(row_count, HQ), first_head, head_part, 1)
    total_heads = lax.dynamic_slice_in_dim(totals.reshape(row_count, HQ), first_head, head_part, 1)
    query_heads = lax.dynamic_slice_in_dim(
        row_values[:, : HQ * DH], first_head * DH, head_part * DH, 1
    )
    query_heads = query_heads.reshape(row_count, head_part, DH).astype(jnp.float32)
    own_keys, own_values = split_kv(row_values[:, HQ * DH :])
    key_heads = lax.dynamic_slice_in_dim(
        jnp.repeat(own_keys, HQ // KVH, axis=1), first_head, head_part, 1
    )
    value_heads = lax.dynamic_slice_in_dim(
        jnp.repeat(own_values, HQ // KVH, axis=1), first_head, head_part, 1
    )
    own_score = jnp.sum(query_heads * key_heads.astype(jnp.float32), axis=-1) * DH ** (-0.5)
    overall = jnp.maximum(high_heads, own_score)
    factor_old = jnp.exp(high_heads - overall)
    factor_own = jnp.exp(own_score - overall)
    denom = total_heads * factor_old + factor_own
    numer = shares.reshape(row_count, head_part, DH) * factor_old[..., None] + factor_own[
        ..., None
    ] * value_heads.astype(jnp.float32)
    return (numer / denom[..., None]).reshape(row_count, head_part * DH).astype(jnp.bfloat16)


def body(beam_rows, route, parent, prefix_kv, pages):
    prompt_count = lax.axis_size("prompt")
    seq_count = lax.axis_size("seq")
    step_count, row_count, piece_width = beam_rows.shape
    slot_cap = 2 * row_count // prompt_count
    slot_total = prompt_count * slot_cap
    full_width = piece_width * seq_count
    prefix_rows = prefix_kv[0]
    outputs = []
    for step_index in range(step_count):
        own_rows = beam_rows[step_index]
        position = slot_positions(route[step_index, :, 0], slot_cap, prompt_count)
        complete = whole_rows(own_rows)
        arrived = lax.all_to_all(
            spread(complete, position, slot_total, prompt_count),
            "prompt",
            split_axis=0,
            concat_axis=0,
            tiled=True,
        )
        received = arrived.reshape(slot_total, full_width)
        prefix_part = shared_partial(received[:, : HQ * DH], prefix_rows)
        parent_pages = jnp.take(pages, parent[step_index], axis=0)
        sent_pages = spread(parent_pages, position, slot_total, prompt_count)
        got_pages = lax.all_to_all(sent_pages, "prompt", split_axis=0, concat_axis=0, tiled=True)
        got_pages = got_pages.reshape((slot_total,) + parent_pages.shape[1:])
        suffix_part = page_partial(received[:, : HQ * DH], got_pages)
        combined = combine_seq(join_parts(prefix_part, suffix_part))
        finished = finish_rows(combined, received, seq_count)
        returned = lax.all_to_all(
            finished.reshape(prompt_count, slot_cap, finished.shape[1]),
            "prompt",
            split_axis=0,
            concat_axis=0,
            tiled=True,
        )
        outputs.append(returned.reshape(slot_total, finished.shape[1])[position])
    return jnp.stack(outputs)


def solution(mesh):
    return jax.shard_map(
        body,
        mesh=mesh,
        in_specs=(
            P(None, "prompt", "seq"),
            P(None, "prompt", None),
            P(None, "prompt"),
            P("prompt", "seq", None),
            P("prompt", "seq", None),
        ),
        out_specs=P(None, "prompt", "seq"),
        check_vma=False,
    )
```

profile of v0, /device:TPU:8, one launch (start us, length us, event | category | flops | bytes accessed | tf_op | source)
XLA Modules:
  0.0 577.7 jit_solution(999279277106219332)
XLA Ops:
  8.6 13.7 %all-gather = bf16[1,64,5120]{2,1,0:T(8,128)(2,1)S(1)} all-gather(bf16[1,64,640]{2,1,0:T(8,128)(2,1)S(1)} %get-tuple-element.38), channel_id=2, replica_groups=mesh['prompt'=64,'seq'=8] {'seq'}, dimensions={2}, use_global_device_ids=true | all-gather | bytes 737280 | tf_op jit(solution)/shard_map/all_gather | solution.py:12
  26.4 16.6 %all-to-all-start = ((bf16[64,2,5120]{2,1,0:T(2,128)(2,1)}), bf16[64,2,5120]{2,1,0:T(2,128)(2,1)S(1)}, u32[]{:S(2)}, u32[]{:S(2)}) async-start(bf16[64,2,5120]{2,1,0:T(2,128)(2,1)} %reshape.231), calls=%async_computation | async-start | bytes 2621440 | tf_op jit(solution)/shard_map/all_to_all | solution.py:125
  43.0 13.3 %all-gather.1 = bf16[1,64,5120]{2,1,0:T(8,128)(2,1)S(1)} all-gather(bf16[1,64,640]{2,1,0:T(8,128)(2,1)S(1)} %get-tuple-element.39), channel_id=3, replica_groups=mesh['prompt'=64,'seq'=8] {'seq'}, dimensions={2}, use_global_device_ids=true | all-gather | bytes 737280 | tf_op jit(solution)/shard_map/all_gather | solution.py:12
  62.9 15.4 %all-to-all-done = bf16[64,2,5120]{2,1,0:T(2,128)(2,1)S(1)} async-done(((bf16[64,2,5120]{2,1,0:T(2,128)(2,1)}), bf16[64,2,5120]{2,1,0:T(2,128)(2,1)S(1)}, u32[]{:S(2)}, u32[]{:S(2)}) %all-to-all-start) | async-done | bytes 1310752 | tf_op jit(solution)/shard_map/all_to_all | solution.py:125
  78.4 8.2 %all-to-all-start.3 = ((bf16[64,2,5120]{2,1,0:T(2,128)(2,1)}), bf16[64,2,5120]{2,1,0:T(2,128)(2,1)}, u32[]{:S(2)}, u32[]{:S(2)}) async-start(bf16[64,2,5120]{2,1,0:T(2,128)(2,1)} %reshape.249), calls=%async_computation.4 | async-start | bytes 2621440 | tf_op jit(solution)/shard_map/all_to_all | solution.py:125
  97.2 9.9 %scatter_fusion = bf16[128,16,1024]{2,1,0:T(8,128)(2,1)} fusion(bf16[128,16,1024]{2,1,0:T(8,128)(2,1)} %broadcast.120.clone.1, s32[64]{0:T(128)S(1)} %get-tuple-element.42, bf16[64,16,1024]{2,1,0:T(8,128)(2,1)} %get-tuple-element.57), kind=kCustom, calls=%fused_computation.5 | custom fusion | bytes 6291712 | tf_op jit(solution)/shard_map/scatter | solution.py:24
  107.1 13.4 %all-to-all-done.3 = bf16[64,2,5120]{2,1,0:T(2,128)(2,1)} async-done(((bf16[64,2,5120]{2,1,0:T(2,128)(2,1)}), bf16[64,2,5120]{2,1,0:T(2,128)(2,1)}, u32[]{:S(2)}, u32[]{:S(2)}) %all-to-all-start.3) | async-done | bytes 1310752 | tf_op jit(solution)/shard_map/all_to_all | solution.py:125
  120.5 7.7 %all-to-all-start.1 = ((bf16[64,2,16,1024]{3,2,1,0:T(8,128)(2,1)}), bf16[64,2,16,1024]{3,2,1,0:T(8,128)(2,1)}, u32[]{:S(2)}, u32[]{:S(2)}) async-start(bf16[64,2,16,1024]{3,2,1,0:T(8,128)(2,1)} %bitcast.119), calls=%async_computation.1 | async-start | bytes 8388608 | tf_op jit(solution)/shard_map/all_to_all | solution.py:136
  130.7 8.6 %scatter_fusion.1 = bf16[128,16,1024]{2,1,0:T(8,128)(2,1)} fusion(bf16[128,16,1024]{2,1,0:T(8,128)(2,1)} %broadcast.120.clone, s32[64]{0:T(128)S(1)} %get-tuple-element.43, bf16[64,16,1024]{2,1,0:T(8,128)(2,1)S(1)} %get-tuple-element.56), kind=kCustom, calls=%fused_computation.7 | custom fusion | bytes 6291712 | tf_op jit(solution)/shard_map/scatter | solution.py:24
  139.3 106.6 %all-to-all-done.1 = bf16[64,2,16,1024]{3,2,1,0:T(8,128)(2,1)} async-done(((bf16[64,2,16,1024]{3,2,1,0:T(8,128)(2,1)}), bf16[64,2,16,1024]{3,2,1,0:T(8,128)(2,1)}, u32[]{:S(2)}, u32[]{:S(2)}) %all-to-all-start.1) | async-done | bytes 4194336 | tf_op jit(solution)/shard_map/all_to_all | solution.py:136
  246.0 31.3 %all-to-all-start.4 = ((bf16[64,2,16,1024]{3,2,1,0:T(8,128)(2,1)}), bf16[64,2,16,1024]{3,2,1,0:T(8,128)(2,1)}, u32[]{:S(2)}, u32[]{:S(2)}) async-start(bf16[64,2,16,1024]{3,2,1,0:T(8,128)(2,1)} %bitcast.118), calls=%async_computation.5 | async-start | bytes 8388608 | tf_op jit(solution)/shard_map/all_to_all | solution.py:136
  294.8 4.6 fusion.38
  304.0 4.7 copy.201
  314.4 74.0 %all-to-all-done.4 = bf16[64,2,16,1024]{3,2,1,0:T(8,128)(2,1)} async-done(((bf16[64,2,16,1024]{3,2,1,0:T(8,128)(2,1)}), bf16[64,2,16,1024]{3,2,1,0:T(8,128)(2,1)}, u32[]{:S(2)}, u32[]{:S(2)}) %all-to-all-start.4) | async-done | bytes 4194336 | tf_op jit(solution)/shard_map/all_to_all | solution.py:136
  388.4 4.8 fusion.39
  397.7 4.6 copy.217
  414.0 4.7 copy.204
  426.2 23.6 %all-reduce.1 = (f32[128,4,8]{0,2,1:T(8,128)S(1)}, f32[128,4,8]{0,2,1:T(8,128)S(1)}) all-reduce(f32[128,4,8]{0,2,1:T(8,128)S(1)} %max.32, f32[128,4,8]{0,2,1:T(8,128)S(1)} %copy-done.18), channel_id=1, replica_groups=mesh['prompt'=64,'seq'=8] {'seq'}, use_global_device_ids=true, to_apply=%region_18.20 | all-reduce | flops 8192 | bytes 65536 | tf_op jit(solution)/shard_map/pmax | solution.py:75
  462.5 4.6 copy.220
  483.6 23.6 %all-reduce = (f32[128,32]{0,1:T(8,128)S(1)}, f32[128,32]{0,1:T(8,128)S(1)}) all-reduce(f32[128,32]{0,1:T(8,128)S(1)} %get-tuple-element.20, f32[128,32]{0,1:T(8,128)S(1)} %copy-done.20), channel_id=1, replica_groups=mesh['prompt'=64,'seq'=8] {'seq'}, use_global_device_ids=true, to_apply=%region_23.25 | all-reduce | flops 8192 | bytes 65536 | tf_op jit(solution)/shard_map/psum | solution.py:77
  510.1 21.8 %all-to-all-start.2 = ((bf16[64,2,512]{2,1,0:T(2,128)(2,1)}), bf16[64,2,512]{2,1,0:T(2,128)(2,1)S(1)}, u32[]{:S(2)}, u32[]{:S(2)}) async-start(bf16[64,2,512]{2,1,0:T(2,128)(2,1)} %convert_element_type.78), calls=%async_computation.3 | async-start | bytes 262144 | tf_op jit(solution)/shard_map/all_to_all | solution.py:141
  532.6 9.3 %reduce-scatter.5.cloned.1.call-done = f32[128,512]{0,1:T(8,128)} async-done(((f32[128,4096]{0,1:T(8,128)}), f32[128,512]{0,1:T(8,128)}) %reduce-scatter.5.cloned.1.call-update) | async-done | bytes 262160 | tf_op jit(solution)/shard_map/reduce_scatter | solution.py:79
  544.1 13.3 %all-to-all-start.5 = ((bf16[64,2,512]{2,1,0:T(2,128)(2,1)}), bf16[64,2,512]{2,1,0:T(2,128)(2,1)S(1)}, u32[]{:S(2)}, u32[]{:S(2)}) async-start(bf16[64,2,512]{2,1,0:T(2,128)(2,1)} %convert_element_type.89), calls=%async_computation.7 | async-start | bytes 262144 | tf_op jit(solution)/shard_map/all_to_all | solution.py:141
  558.3 10.9 %all-to-all-done.5 = bf16[64,2,512]{2,1,0:T(2,128)(2,1)S(1)} async-done(((bf16[64,2,512]{2,1,0:T(2,128)(2,1)}), bf16[64,2,512]{2,1,0:T(2,128)(2,1)S(1)}, u32[]{:S(2)}, u32[]{:S(2)}) %all-to-all-start.5) | async-done | bytes 131104 | tf_op jit(solution)/shard_map/all_to_all | solution.py:141
  (151 shorter events, 113.9 us)
Async XLA Ops:
  6.5 80.1 %copy-start = (bf16[32,16,1024]{2,1,0:T(8,128)(2,1)S(1)}, bf16[32,16,1024]{2,1,0:T(8,128)(2,1)}, u32[]{:S(2)}) copy-start(bf16[32,16,1024]{2,1,0:T(8,128)(2,1)} %param.11) | copy-start | bytes 3145732
  23.1 74.0 %copy-start.25 = (s32[64]{0:T(128)}, s32[64]{0:T(128)S(1)}, u32[]{:S(2)}) copy-start(s32[64]{0:T(128)S(1)} %get-tuple-element.42) | copy-start | bytes 772
  23.1 107.6 %copy-start.23 = (s32[64]{0:T(128)}, s32[64]{0:T(128)S(1)}, u32[]{:S(2)}) copy-start(s32[64]{0:T(128)S(1)} %get-tuple-element.43) | copy-start | bytes 772
  26.4 51.9 %all-to-all-start = ((bf16[64,2,5120]{2,1,0:T(2,128)(2,1)}), bf16[64,2,5120]{2,1,0:T(2,128)(2,1)S(1)}, u32[]{:S(2)}, u32[]{:S(2)}) async-start(bf16[64,2,5120]{2,1,0:T(2,128)(2,1)} %reshape.231), calls=%async_computation | async-start | bytes 2621440 | tf_op jit(solution)/shard_map/all_to_all | solution.py:125
  59.1 27.5 %copy-start.27 = (s32[2,64]{1,0:T(2,128)S(1)}, s32[2,64]{1,0:T(2,128)}, u32[]{:S(2)}) copy-start(s32[2,64]{1,0:T(2,128)} %param.9) | copy-start | bytes 1540
  78.4 10.3 %copy-start.6 = (bf16[64,2,5120]{2,1,0:T(2,128)(2,1)}, bf16[64,2,5120]{2,1,0:T(2,128)(2,1)S(1)}, u32[]{:S(2)}) copy-start(bf16[64,2,5120]{2,1,0:T(2,128)(2,1)S(1)} %all-to-all-done) | copy-start | bytes 3932164
  78.4 42.1 %all-to-all-start.3 = ((bf16[64,2,5120]{2,1,0:T(2,128)(2,1)}), bf16[64,2,5120]{2,1,0:T(2,128)(2,1)}, u32[]{:S(2)}, u32[]{:S(2)}) async-start(bf16[64,2,5120]{2,1,0:T(2,128)(2,1)} %reshape.249), calls=%async_computation.4 | async-start | bytes 2621440 | tf_op jit(solution)/shard_map/all_to_all | solution.py:125
  120.5 125.5 %all-to-all-start.1 = ((bf16[64,2,16,1024]{3,2,1,0:T(8,128)(2,1)}), bf16[64,2,16,1024]{3,2,1,0:T(8,128)(2,1)}, u32[]{:S(2)}, u32[]{:S(2)}) async-start(bf16[64,2,16,1024]{3,2,1,0:T(8,128)(2,1)} %bitcast.119), calls=%async_computation.1 | async-start | bytes 8388608 | tf_op jit(solution)/shard_map/all_to_all | solution.py:136
  246.0 31.4 %copy-start.15 = (bf16[1,128,1024]{2,1,0:T(8,128)(2,1)S(1)}, bf16[1,128,1024]{2,1,0:T(8,128)(2,1)}, u32[]{:S(2)}) copy-start(bf16[1,128,1024]{2,1,0:T(8,128)(2,1)} %param.10) | copy-start | bytes 786436
  246.0 142.5 %all-to-all-start.4 = ((bf16[64,2,16,1024]{3,2,1,0:T(8,128)(2,1)}), bf16[64,2,16,1024]{3,2,1,0:T(8,128)(2,1)}, u32[]{:S(2)}, u32[]{:S(2)}) async-start(bf16[64,2,16,1024]{3,2,1,0:T(8,128)(2,1)} %bitcast.118), calls=%async_computation.5 | async-start | bytes 8388608 | tf_op jit(solution)/shard_map/all_to_all | solution.py:136
  277.3 230.7 %reduce-scatter.3.cloned.1.call-start = ((), (), s32[]{:S(2)}) async-start(), calls=%async_computation.8 | async-start | bytes 2359296 | tf_op jit(solution)/shard_map/reduce_scatter | solution.py:79
  313.0 80.2 %copy-start.10 = (f32[128,4,8]{2,1,0:T(4,128)}, f32[128,4,8]{2,1,0:T(4,128)S(1)}, u32[]{:S(2)}) copy-start(f32[128,4,8]{2,1,0:T(4,128)S(1)} %get-tuple-element.52) | copy-start | bytes 49156
  313.1 80.1 %copy-start.16 = (f32[128,4,8]{0,2,1:T(8,128)}, f32[128,4,8]{0,2,1:T(8,128)S(1)}, u32[]{:S(2)}) copy-start(f32[128,4,8]{0,2,1:T(8,128)S(1)} %copy.202) | copy-start | bytes 49156
  423.2 26.7 %copy-start.14 = (f32[128,4,8]{0,2,1:T(8,128)S(1)}, f32[128,4,8]{0,2,1:T(8,128)}, u32[]{:S(2)}) copy-start(f32[128,4,8]{0,2,1:T(8,128)} %copy-done.13) | copy-start | bytes 49156
  423.2 26.7 %copy-start.17 = (f32[128,4,8]{0,2,1:T(8,128)S(1)}, f32[128,4,8]{0,2,1:T(8,128)}, u32[]{:S(2)}) copy-start(f32[128,4,8]{0,2,1:T(8,128)} %copy-done.16) | copy-start | bytes 49156
  423.2 26.7 %copy-start.19 = (f32[128,4,8]{0,2,1:T(8,128)S(1)}, f32[128,4,8]{0,2,1:T(8,128)}, u32[]{:S(2)}) copy-start(f32[128,4,8]{0,2,1:T(8,128)} %convert_reduce_fusion.3) | copy-start | bytes 49156
  449.9 4.9 copy-start.22
  449.9 24.7 %copy-start.21 = (f32[128,4,8]{0,2,1:T(8,128)}, f32[128,4,8]{0,2,1:T(8,128)S(1)}, u32[]{:S(2)}) copy-start(f32[128,4,8]{0,2,1:T(8,128)S(1)} %get-tuple-element.8) | copy-start | bytes 49156
  454.8 87.2 %reduce-scatter.5.cloned.1.call-start = ((), (), s32[]{:S(2)}) async-start(), calls=%async_computation.9 | async-start | bytes 2359296 | tf_op jit(solution)/shard_map/reduce_scatter | solution.py:79
  508.2 49.2 %copy-start.26 = (s32[64]{0:T(128)S(1)}, s32[64]{0:T(128)}, u32[]{:S(2)}) copy-start(s32[64]{0:T(128)} %copy-done.25) | copy-start | bytes 772
  508.2 49.3 %copy-start.24 = (s32[64]{0:T(128)S(1)}, s32[64]{0:T(128)}, u32[]{:S(2)}) copy-start(s32[64]{0:T(128)} %copy-done.23) | copy-start | bytes 772
  510.1 34.0 %all-to-all-start.2 = ((bf16[64,2,512]{2,1,0:T(2,128)(2,1)}), bf16[64,2,512]{2,1,0:T(2,128)(2,1)S(1)}, u32[]{:S(2)}, u32[]{:S(2)}) async-start(bf16[64,2,512]{2,1,0:T(2,128)(2,1)} %convert_element_type.78), calls=%async_computation.3 | async-start | bytes 262144 | tf_op jit(solution)/shard_map/all_to_all | solution.py:141
  541.9 28.7 %copy-start.1 = (bf16[32,16,1024]{2,1,0:T(8,128)(2,1)S(1)}, bf16[32,16,1024]{2,1,0:T(8,128)(2,1)}, u32[]{:S(2)}) copy-start(bf16[32,16,1024]{2,1,0:T(8,128)(2,1)} %param.11) | copy-start | bytes 3145732
  544.1 25.1 %all-to-all-start.5 = ((bf16[64,2,512]{2,1,0:T(2,128)(2,1)}), bf16[64,2,512]{2,1,0:T(2,128)(2,1)S(1)}, u32[]{:S(2)}, u32[]{:S(2)}) async-start(bf16[64,2,512]{2,1,0:T(2,128)(2,1)} %convert_element_type.89), calls=%async_computation.7 | async-start | bytes 262144 | tf_op jit(solution)/shard_map/all_to_all | solution.py:141
  (12 other events, 33.2 us)
Sparse Core Ops, SparseCore 0:
  454.9 46.0 reduce-scatter.2
  503.8 38.0 reduce-scatter.4
where the time goes:
time: 587 us; the launch traced here: 578 us
  waiting for transfers between devices  230 us (39%)
  local copies, waits for them, and re-layouts  115 us (20%)
  starting transfers between devices  99 us (17%)
  blocking collectives  74.3 us (13%)
  matrix products  26.1 us (4%)
  other arithmetic  19.4 us (3%)
  between operations  14.1 us (2%)
    all_to_all x2, waiting for transfers between devices, body(): lax.all_to_all(sent_pages, 'prompt', split_axis=0, concat_axis=0, tiled=T...  181 us
    all_to_all x2, starting transfers between devices, body(): lax.all_to_all(sent_pages, 'prompt', split_axis=0, concat_axis=0, tiled=T...  39 us
    all_to_all x2, starting transfers between devices, body(): lax.all_to_all(finished.reshape(prompt_count, slot_cap, finished.shape[1]...  35.1 us
    all_to_all x2, waiting for transfers between devices, body(): lax.all_to_all(spread(complete, position, slot_total, prompt_count), 'pro...  28.9 us
    all_gather x2, blocking collectives, whole_rows(): return lax.all_gather(pieces, 'seq', axis=1, tiled=True)  27 us
    all_to_all x2, starting transfers between devices, body(): lax.all_to_all(spread(complete, position, slot_total, prompt_count), 'pro...  24.8 us
    psum x1, blocking collectives, combine_seq(): totals = lax.psum(parts[1] * factor, 'seq')  23.6 us
    pmax x1, blocking collectives, combine_seq(): highest = lax.pmax(parts[0], 'seq')  23.6 us
  transfers between devices with their start and end apart: 8, of which 6 were waited for; matrix products, arithmetic and copies ran while one was open for 19% of the time, Pallas kernels for 0%

commit v1 on v0

v1 whole, which is shorter than its diff:
```python
import jax
import jax.numpy as jnp
from jax import lax
from jax.experimental import pallas as pl
from jax.experimental.pallas import tpu as pltpu
from jax.sharding import PartitionSpec as P

HQ = 32
KVH = 4
DH = 128
CAP = 2
SCALE = DH ** (-0.5)
BF = jnp.bfloat16
F32 = jnp.float32
NT = (((1,), (1,)), ((), ()))
NN = (((1,), (0,)), ((), ()))
TN = (((0,), (0,)), ((), ()))
VMEM = pl.BlockSpec(memory_space=pltpu.VMEM)
SMEM = pl.BlockSpec(memory_space=pltpu.SMEM)


def dot(a, b, dims):
    return lax.dot_general(a, b, dims, preferred_element_type=F32)


def call(kernel, outs, in_specs, scratch=(), flops=0, nbytes=0, name=None):
    return pl.pallas_call(
        kernel,
        out_shape=outs,
        in_specs=in_specs,
        out_specs=jax.tree.map(lambda _: VMEM, outs),
        scratch_shapes=list(scratch),
        compiler_params=pltpu.CompilerParams(vmem_limit_bytes=40 * 1024 * 1024),
        cost_estimate=pl.CostEstimate(flops=flops, bytes_accessed=nbytes, transcendentals=0),
        name=name,
    )


def slots_kernel(seq_ref, own_ref, near_ref, far_ref, rcol_ref, rrow_ref, sent_ref, query_ref, line):
    rows = own_ref.shape[0]
    width = own_ref.shape[1]
    half = rows // 2
    line[:, :width] = far_ref[...]
    line[:, width : 2 * width] = near_ref[...]
    line[:, 2 * width :] = own_ref[...]
    first = pl.multiple_of((10 - seq_ref[0]) * DH, DH)
    query = line[:, pl.ds(first, query_ref.shape[1])]
    query_ref[...] = query
    before = lax.broadcasted_iota(jnp.int32, (rows, rows), 0)
    after = lax.broadcasted_iota(jnp.int32, (rows, rows), 1)
    same = (rcol_ref[...] == rrow_ref[...]) & (before < after) & ((before < half) == (after < half))
    rank = jnp.sum(same.astype(jnp.int32), axis=0, keepdims=True)
    step = (lax.broadcasted_iota(jnp.int32, (1, rows), 1) >= half).astype(jnp.int32)
    position = rrow_ref[...] * (2 * CAP) + step * CAP + rank
    slot = lax.broadcasted_iota(jnp.int32, (sent_ref.shape[0], rows), 0)
    onehot = (slot == position).astype(F32).astype(BF)
    sent_ref[...] = dot(onehot, query, NN).astype(BF)


def thirds(value):
    high = value.astype(BF).astype(F32)
    rest = value - high
    middle = rest.astype(BF).astype(F32)
    low = (rest - middle).astype(BF).astype(F32)
    return [high, middle, low]


def prefix_kernel(query_ref, kv_ref, out_ref):
    slots = query_ref.shape[0]
    blocks = kv_ref.shape[0]
    heads = query_ref.shape[1] // DH
    values_t = [kv_ref[b, :, DH:].astype(F32).T.astype(BF) for b in range(blocks)]
    stats = []
    for h in range(heads):
        query = query_ref[:, h * DH : (h + 1) * DH]
        tops, totals, parts = [], [], []
        for b in range(blocks):
            scores = dot(kv_ref[b, :, :DH], query, NT) * SCALE
            top = jnp.max(scores, axis=0, keepdims=True)
            weights = jnp.exp(scores - top).astype(BF)
            tops.append(top)
            totals.append(jnp.sum(weights.astype(F32), axis=0, keepdims=True))
            parts.append(dot(values_t[b], weights, NN))
        top = tops[0]
        for b in range(1, blocks):
            top = jnp.maximum(top, tops[b])
        total = jnp.zeros_like(top)
        mixed = jnp.zeros((DH, slots), F32)
        for b in range(blocks):
            factor = jnp.exp(tops[b] - top)
            total += totals[b] * factor
            mixed += parts[b] * factor
        mixed = mixed / total
        out_ref[:, h * DH : (h + 1) * DH] = mixed.T.astype(BF)
        stats += thirds(top) + thirds(total) + [jnp.zeros_like(top)] * 2
    stats.append(jnp.zeros((DH - len(stats), slots), F32))
    out_ref[:, heads * DH :] = jnp.concatenate(stats, axis=0).T.astype(BF)


def page_kernel(seq_ref, query_ref, parent_ref, mine_ref, other_ref, out_ref, stat_ref):
    rows = query_ref.shape[0]
    heads = query_ref.shape[1] // DH
    senders = mine_ref.shape[0]
    page_rows = mine_ref.shape[1] - rows
    seg = DH // (2 * senders)
    page_count = page_rows // seg
    query = jnp.concatenate([query_ref[:, h * DH : (h + 1) * DH] for h in range(heads)], axis=0)
    parent = jnp.concatenate([parent_ref[...]] * heads, axis=1)

    def page(j, first):
        at = pl.ds(pl.multiple_of(j * seg, seg), seg)
        return jnp.concatenate(
            [ref[x, at, first : first + DH] for ref in (mine_ref, other_ref) for x in range(senders)], axis=0
        )

    def score(j, held):
        return jnp.where(parent == j, dot(page(j, 0), query, NT), held)

    scores = lax.fori_loop(0, page_count, score, jnp.zeros((DH, heads * rows), F32)) * SCALE
    top = jnp.max(scores, axis=0, keepdims=True)
    weights = jnp.exp(scores - top).astype(BF).astype(F32)
    total = jnp.sum(weights, axis=0, keepdims=True)

    def weigh(j, held):
        chosen = jnp.where(parent == j, weights, 0.0).astype(BF)
        return held + dot(page(j, DH), chosen, TN)

    mixed = lax.fori_loop(0, page_count, weigh, jnp.zeros((DH, heads * rows), F32))
    stats = [top[:, h * rows : (h + 1) * rows] for h in range(heads)]
    stats += [total[:, h * rows : (h + 1) * rows] for h in range(heads)]
    stats.append(jnp.zeros((DH - 2 * heads, rows), F32))
    stats = jnp.concatenate(stats, axis=0).T
    place = seq_ref[0]
    even_core = lax.rem(place, 2) == 0
    mine = mine_ref[senders - 1, page_rows:, :]
    other = other_ref[senders - 1, page_rows:, :]
    even = jnp.where(even_core, mine, other)
    odd = jnp.where(even_core, other, mine)
    own_key = jnp.where(place // 2 < senders - 1, even[:, :DH], odd[:, :DH]).astype(F32)
    own_value = odd[:, DH:].astype(F32)
    lane = lax.broadcasted_iota(jnp.int32, (rows, DH), 1)
    packed = jnp.zeros((rows, DH), F32)
    for h in range(heads):
        cols = slice(h * DH, (h + 1) * DH)
        own_score = jnp.sum(query_ref[:, cols].astype(F32) * own_key, axis=1, keepdims=True) * SCALE
        page_top = stats[:, h : h + 1]
        best = jnp.maximum(page_top, own_score)
        factor_page = jnp.exp(page_top - best)
        factor_own = jnp.exp(own_score - best)
        both = stats[:, heads + h : heads + h + 1] * factor_page + factor_own
        part = mixed[:, h * rows : (h + 1) * rows].T
        out_ref[:, cols] = part * factor_page + factor_own * own_value
        packed = jnp.where(lane == h, best, packed)
        packed = jnp.where(lane == heads + h, both, packed)
    stat_ref[...] = packed


def finish_kernel(back_ref, rcol_ref, rrow_ref, part_ref, stat_ref, out_ref):
    rows = part_ref.shape[0]
    half = rows // 2
    heads = part_ref.shape[1] // DH
    this = lax.broadcasted_iota(jnp.int32, (rows, rows), 0)
    before = lax.broadcasted_iota(jnp.int32, (rows, rows), 1)
    same = (rcol_ref[...] == rrow_ref[...]) & (before < this) & ((before < half) == (this < half))
    rank = jnp.sum(same.astype(jnp.int32), axis=1, keepdims=True)
    step = (lax.broadcasted_iota(jnp.int32, (rows, 1), 0) >= half).astype(jnp.int32)
    position = rcol_ref[...] * (2 * CAP) + step * CAP + rank
    slot = lax.broadcasted_iota(jnp.int32, (rows, back_ref.shape[0]), 1)
    onehot = (slot == position).astype(F32).astype(BF)
    got = dot(onehot, back_ref[...], NN)
    stats = stat_ref[...]
    for h in range(heads):
        cols = slice(h * DH, (h + 1) * DH)
        at = heads * DH + 8 * h
        prefix_top = got[:, at : at + 1] + got[:, at + 1 : at + 2] + got[:, at + 2 : at + 3]
        prefix_total = got[:, at + 3 : at + 4] + got[:, at + 4 : at + 5] + got[:, at + 5 : at + 6]
        home_top = stats[:, h : h + 1]
        home_total = stats[:, heads + h : heads + h + 1]
        best = jnp.maximum(prefix_top, home_top)
        factor_prefix = jnp.exp(prefix_top - best) * prefix_total
        factor_home = jnp.exp(home_top - best)
        denom = factor_prefix + home_total * factor_home
        numer = got[:, cols] * factor_prefix + part_ref[:, cols] * factor_home
        out_ref[:, cols] = (numer / denom).astype(BF)


def by_head(tokens):
    count = tokens.shape[0]
    return tokens.reshape(count, 2, KVH, DH).transpose(2, 0, 1, 3).reshape(KVH, count, 2 * DH)


def body(beam_rows, route, parent, prefix_kv, pages):
    prompt_count = lax.axis_size("prompt")
    seq_count = lax.axis_size("seq")
    step_count, row_count, width = beam_rows.shape
    rows = step_count * row_count
    head_part = HQ // seq_count
    out_width = head_part * DH
    slots = prompt_count * step_count * CAP
    place = lax.axis_index("seq").astype(jnp.int32).reshape(1)
    own = beam_rows.reshape(rows, width)
    route_col = route.reshape(rows, 1)
    route_row = route.reshape(1, rows)

    with jax.named_scope("rows_to_heads"):
        near = lax.ppermute(own, "seq", [(i, i + 1) for i in range(seq_count - 1)])
        far = lax.ppermute(own, "seq", [(4, 6), (5, 7)])
    with jax.named_scope("prefix_to_heads"):
        prefix = jnp.repeat(by_head(prefix_kv[0]), 2, axis=0)
        prefix = lax.all_to_all(prefix, "seq", 0, 0, tiled=True)
    with jax.named_scope("slots"):
        sent, query = call(
            slots_kernel,
            (jax.ShapeDtypeStruct((slots, out_width), BF), jax.ShapeDtypeStruct((rows, out_width), BF)),
            [SMEM] + [VMEM] * 5,
            [pltpu.VMEM((rows, 3 * width), BF)],
            flops=2 * slots * rows * out_width,
            nbytes=1 << 20,
        )(place, own, near, far, route_col, route_row)
    with jax.named_scope("rows_out"):
        sent = sent.reshape(prompt_count, step_count * CAP, out_width)
        arrived = lax.all_to_all(sent, "prompt", 0, 0, tiled=True).reshape(slots, out_width)
    with jax.named_scope("pages_to_heads"):
        piece = [own[:, c * DH : (c + 1) * DH] for c in range(5)]
        own_kv = jnp.stack(
            [jnp.concatenate([piece[k], piece[v]], axis=1) for k, v in ((2, 1), (3, 2), (4, 3), (0, 4))]
        )
        outgoing = jnp.concatenate([by_head(pages.reshape(-1, pages.shape[2])), own_kv], axis=1)
        groups = [list(range(core, seq_count, 2)) for core in range(2)]
        mine = lax.all_to_all(outgoing, "seq", 0, 0, tiled=True, axis_index_groups=groups)
        other = lax.ppermute(mine, "seq", [(i, i ^ 1) for i in range(seq_count)])
    with jax.named_scope("prefix_part"):
        part = call(
            prefix_kernel,
            jax.ShapeDtypeStruct((slots, out_width + DH), BF),
            [VMEM] * 2,
            flops=4 * slots * head_part * seq_count * DH * DH,
            nbytes=1 << 20,
        )(arrived, prefix)
    with jax.named_scope("rows_back"):
        part = part.reshape(prompt_count, step_count * CAP, out_width + DH)
        back = lax.all_to_all(part, "prompt", 0, 0, tiled=True).reshape(slots, out_width + DH)
    with jax.named_scope("page_part"):
        home, home_stats = call(
            page_kernel,
            (jax.ShapeDtypeStruct((rows, out_width), F32), jax.ShapeDtypeStruct((rows, DH), F32)),
            [SMEM] + [VMEM] * 4,
            flops=4 * rows * head_part * 4096 * DH,
            nbytes=4 << 20,
        )(place, query, parent.reshape(1, rows), mine, other)
    with jax.named_scope("finish"):
        attended = call(
            finish_kernel,
            jax.ShapeDtypeStruct((rows, out_width), BF),
            [VMEM] * 5,
            flops=2 * slots * rows * out_width,
            nbytes=1 << 20,
        )(back, route_col, route_row, home, home_stats)
    return attended.reshape(step_count, row_count, out_width)


def solution(mesh):
    return jax.shard_map(
        body,
        mesh=mesh,
        in_specs=(
            P(None, "prompt", "seq"),
            P(None, "prompt", None),
            P(None, "prompt"),
            P("prompt", "seq", None),
            P("prompt", "seq", None),
        ),
        out_specs=P(None, "prompt", "seq"),
        check_vma=False,
    )
```

time: 587 us -> 120 us (0.20)
  the two profiles are of different devices: /device:TPU:8 before, /device:TPU:16 now
where the time goes in v1:
time: 120 us
  waiting for transfers between devices  50.3 us (42%)
  starting transfers between devices  39 us (32%)
  Pallas kernels  20.5 us (17%)
  local copies, waits for them, and re-layouts  7.88 us (7%)
  other arithmetic  1.84 us (2%)
    all_to_all x1, starting transfers between devices, body(): lax.all_to_all(sent, 'prompt', 0, 0, tiled=True).reshape(slots, out_width)  16.5 us
    pallas_call x1, Pallas kernels, body(): call(page_kernel, (jax.ShapeDtypeStruct((rows, out_width), F32), jax.Shap...  16.3 us
    all_to_all x1, waiting for transfers between devices, body(): lax.all_to_all(part, 'prompt', 0, 0, tiled=True)  15.3 us
    all_to_all x1, waiting for transfers between devices, body(): lax.all_to_all(outgoing, 'seq', 0, 0, tiled=True, axis_index_groups=groups)  14.6 us
    all_to_all x1, waiting for transfers between devices, body(): prefix = lax.all_to_all(prefix, 'seq', 0, 0, tiled=True)  10.3 us
    all_to_all x1, waiting for transfers between devices, body(): lax.all_to_all(sent, 'prompt', 0, 0, tiled=True).reshape(slots, out_width)  10.1 us
    all_to_all x1, starting transfers between devices, body(): prefix = lax.all_to_all(prefix, 'seq', 0, 0, tiled=True)  8.25 us
    all_to_all x1, starting transfers between devices, body(): lax.all_to_all(part, 'prompt', 0, 0, tiled=True)  5.65 us
  transfers between devices with their start and end apart: 7, of which 4 were waited for; matrix products, arithmetic and copies ran while one was open for 4% of the time, Pallas kernels for 2%

profile of v1, /device:TPU:16, one launch (start us, length us, event | category | flops | bytes accessed | tf_op | source)
XLA Modules:
  0.0 119.7 jit_solution(2083836350198364200)
XLA Ops:
  0.0 0.8 fusion
  0.8 1.8 %reshape.53 = bf16[512,2,4,128]{3,2,1,0:T(4,128)(2,1)S(1)} reshape(bf16[32,16,1024]{2,1,0:T(8,128)(2,1)} %param.9) | data formatting | bytes 2097152 | tf_op jit(solution)/shard_map/pages_to_heads/reshape;pages_to_heads/reshape | solution.py:189
  2.6 0.8 copy.20
  3.5 0.7 reshape.54
  4.2 1.2 maximum_maximum_fusion
  5.4 4.4 %all-to-all-start.3 = ((bf16[4,640,256]{2,1,0:T(8,128)(2,1)}), bf16[4,640,256]{2,1,0:T(8,128)(2,1)S(1)}, u32[]{:S(2)}, u32[]{:S(2)}) async-start(bf16[4,640,256]{2,1,0:T(8,128)(2,1)} %maximum_maximum_fusion), calls=%async_computation.3 | async-start | bytes 2621440 | tf_op jit(solution)/shard_map/pages_to_heads/all_to_all | solution.py:230
  9.8 1.6 %collective-permute-start = (bf16[128,640]{1,0:T(8,128)(2,1)S(1)}, bf16[128,640]{1,0:T(8,128)(2,1)S(1)}, u32[]{:S(2)}, u32[]{:S(2)}) collective-permute-start(bf16[128,640]{1,0:T(8,128)(2,1)S(1)} %bitcast.22), channel_id=1, source_target_pairs={{0,1},{1,2},{2,3},{3,4},{4,5},{5,6},{6,7},{8,9},{9,10},{10,11},{11... | collective-permute-start | bytes 491528 | tf_op jit(solution)/shard_map/rows_to_heads/ppermute | solution.py:206
  11.4 0.7 collective-permute-start.1
  12.1 0.5 broadcast.5
  12.6 0.7 reduce.5
  13.8 0.8 reshape.46
  14.6 14.6 %all-to-all-done.3.mine_ref = bf16[4,640,256]{2,1,0:T(8,128)(2,1)S(1)} async-done(((bf16[4,640,256]{2,1,0:T(8,128)(2,1)}), bf16[4,640,256]{2,1,0:T(8,128)(2,1)S(1)}, u32[]{:S(2)}, u32[]{:S(2)}) %all-to-all-start.3) | async-done | bytes 1310752 | tf_op jit(solution)/shard_map/pages_to_heads/all_to_all | solution.py:230
  29.2 16.5 %all-to-all-start = ((bf16[64,4,512]{2,1,0:T(4,128)(2,1)}), bf16[64,4,512]{2,1,0:T(4,128)(2,1)S(1)}, u32[]{:S(2)}, u32[]{:S(2)}) async-start(bf16[64,4,512]{2,1,0:T(4,128)(2,1)} %reshape.46), calls=%async_computation | async-start | bytes 524288 | tf_op jit(solution)/shard_map/rows_out/all_to_all | solution.py:222
  45.6 1.9 %collective-permute-start.2 = (bf16[4,640,256]{2,1,0:T(8,128)(2,1)S(1)}, bf16[4,640,256]{2,1,0:T(8,128)(2,1)}, u32[]{:S(2)}, u32[]{:S(2)}) collective-permute-start(bf16[4,640,256]{2,1,0:T(8,128)(2,1)S(1)} %all-to-all-done.3.mine_ref), channel_id=1, source_target_pairs={{0,1},{1,0},{2,3},{3,2},{4,5},{5,4},{6,7},{7,6},{8,9},{9,8},{10,11... | collective-permute-start | bytes 3932168 | tf_op jit(solution)/shard_map/pages_to_heads/ppermute | solution.py:231
  47.9 10.1 %all-to-all-done = bf16[64,4,512]{2,1,0:T(4,128)(2,1)S(1)} async-done(((bf16[64,4,512]{2,1,0:T(4,128)(2,1)}), bf16[64,4,512]{2,1,0:T(4,128)(2,1)S(1)}, u32[]{:S(2)}, u32[]{:S(2)}) %all-to-all-start) | async-done | bytes 262176 | tf_op jit(solution)/shard_map/rows_out/all_to_all | solution.py:222
  58.0 0.8 broadcast_in_dim.3
  58.9 8.3 %all-to-all-start.1 = ((bf16[8,128,256]{2,1,0:T(8,128)(2,1)}), bf16[8,128,256]{2,1,0:T(8,128)(2,1)S(1)}, u32[]{:S(2)}, u32[]{:S(2)}) async-start(bf16[8,128,256]{2,1,0:T(8,128)(2,1)} %bitcast.5), calls=%async_computation.1 | async-start | bytes 1048576 | tf_op jit(solution)/shard_map/prefix_to_heads/all_to_all | solution.py:210
  67.2 10.3 %all-to-all-done.1.kv_ref = bf16[8,128,256]{2,1,0:T(8,128)(2,1)S(1)} async-done(((bf16[8,128,256]{2,1,0:T(8,128)(2,1)}), bf16[8,128,256]{2,1,0:T(8,128)(2,1)S(1)}, u32[]{:S(2)}, u32[]{:S(2)}) %all-to-all-start.1) | async-done | bytes 524320 | tf_op jit(solution)/shard_map/prefix_to_heads/all_to_all | solution.py:210
  77.5 2.3 %prefix_part.1 = bf16[256,640]{1,0:T(8,128)(2,1)S(1)} custom-call(bf16[256,512]{1,0:T(8,128)(2,1)S(1)} %reshape.47.query_ref, bf16[8,128,256]{2,1,0:T(8,128)(2,1)S(1)} %all-to-all-done.1.kv_ref), custom_call_target="tpu_custom_call" | custom-call | flops 536870912 | bytes 1048576 | tf_op jit(solution)/shard_map/prefix_part/pallas_call | solution.py:233
  79.7 0.8 reshape.50
  80.5 5.6 %all-to-all-start.2 = ((bf16[64,4,640]{2,1,0:T(4,128)(2,1)}), bf16[64,4,640]{2,1,0:T(4,128)(2,1)S(1)}, u32[]{:S(2)}, u32[]{:S(2)}) async-start(bf16[64,4,640]{2,1,0:T(4,128)(2,1)} %reshape.50), calls=%async_computation.2 | async-start | bytes 655360 | tf_op jit(solution)/shard_map/rows_back/all_to_all | solution.py:242
  86.3 15.3 %all-to-all-done.2 = bf16[64,4,640]{2,1,0:T(4,128)(2,1)S(1)} async-done(((bf16[64,4,640]{2,1,0:T(4,128)(2,1)}), bf16[64,4,640]{2,1,0:T(4,128)(2,1)S(1)}, u32[]{:S(2)}, u32[]{:S(2)}) %all-to-all-start.2) | async-done | bytes 327712 | tf_op jit(solution)/shard_map/rows_back/all_to_all | solution.py:242
  101.7 16.3 %page_part.1 = (f32[128,512]{1,0:T(8,128)S(1)}, f32[128,128]{1,0:T(8,128)S(1)}) custom-call(s32[1]{0:T(128)} %bitcast.seq_ref, bf16[128,512]{1,0:T(8,128)(2,1)S(1)} %get-tuple-element.10.query_ref, s32[1,128]{1,0:T(1,128)S(1)} %reshape.52.parent_ref, bf16[4,640,256]{2,1,0:T(8,128)(2,1)S(1)} %all-to-all-done.3.mine_ref, ...), custom_call_target="tpu_custom_call" | custom-call | flops 1073741824 | bytes 4194304 | tf_op jit(solution)/shard_map/page_part/pallas_call | solution.py:244
  118.0 1.7 %finish.1 = bf16[128,512]{1,0:T(8,128)(2,1)} custom-call(bf16[256,640]{1,0:T(8,128)(2,1)S(1)} %reshape.51.back_ref, s32[128,1]{1,0:T(8,128)S(1)} %reshape.56.rcol_ref, s32[1,128]{1,0:T(1,128)S(1)} %reshape.45.rrow_ref, f32[128,512]{1,0:T(8,128)S(1)} %get-tuple-element.11.part_ref, f32[128,128]{1,0:T(8,128)S(1)} %get-tuple-element.12.stat_ref), custom_call_target="tpu_custom_call" | custom-call | flops 33554432 | bytes 1048576 | tf_op jit(solution)/shard_map/finish/pallas_call | solution.py:252
  (21 shorter events, 1.1 us)
Async XLA Ops:
  5.4 4.4 %copy-start = (bf16[2,64,640]{2,1,0:T(8,128)(2,1)S(1)}, bf16[2,64,640]{2,1,0:T(8,128)(2,1)}, u32[]{:S(2)}) copy-start(bf16[2,64,640]{2,1,0:T(8,128)(2,1)} %param.5) | copy-start | bytes 491524
  5.4 7.2 %copy-start.2 = (s32[2,64,1]{1,2,0:T(1,128)S(1)}, s32[2,64,1]{1,2,0:T(1,128)}, u32[]{:S(2)}) copy-start(s32[2,64,1]{1,2,0:T(1,128)} %param.6) | copy-start | bytes 1540
  5.4 23.8 %all-to-all-start.3 = ((bf16[4,640,256]{2,1,0:T(8,128)(2,1)}), bf16[4,640,256]{2,1,0:T(8,128)(2,1)S(1)}, u32[]{:S(2)}, u32[]{:S(2)}) async-start(bf16[4,640,256]{2,1,0:T(8,128)(2,1)} %maximum_maximum_fusion), calls=%async_computation.3 | async-start | bytes 2621440 | tf_op jit(solution)/shard_map/pages_to_heads/all_to_all | solution.py:230
  9.8 37.8 %copy-start.1 = (bf16[1,128,1024]{2,1,0:T(8,128)(2,1)S(1)}, bf16[1,128,1024]{2,1,0:T(8,128)(2,1)}, u32[]{:S(2)}) copy-start(bf16[1,128,1024]{2,1,0:T(8,128)(2,1)} %param.8) | copy-start | bytes 786436
  9.8 3.7 %collective-permute-start = (bf16[128,640]{1,0:T(8,128)(2,1)S(1)}, bf16[128,640]{1,0:T(8,128)(2,1)S(1)}, u32[]{:S(2)}, u32[]{:S(2)}) collective-permute-start(bf16[128,640]{1,0:T(8,128)(2,1)S(1)} %bitcast.22), channel_id=1, source_target_pairs={{0,1},{1,2},{2,3},{3,4},{4,5},{5,6},{6,7},{8,9},{9,10},{10,11},{11... | collective-permute-start | bytes 491528 | tf_op jit(solution)/shard_map/rows_to_heads/ppermute | solution.py:206
  11.4 2.1 %collective-permute-start.1 = (bf16[128,640]{1,0:T(8,128)(2,1)S(1)}, bf16[128,640]{1,0:T(8,128)(2,1)S(1)}, u32[]{:S(2)}, u32[]{:S(2)}) collective-permute-start(bf16[128,640]{1,0:T(8,128)(2,1)S(1)} %bitcast.23), channel_id=1, source_target_pairs={{4,6},{5,7},{12,14},{13,15},{20,22},{21,23},{28,30},{29,31},{36,38... | collective-permute-start | bytes 491528 | tf_op jit(solution)/shard_map/rows_to_heads/ppermute | solution.py:207
  29.2 28.9 %all-to-all-start = ((bf16[64,4,512]{2,1,0:T(4,128)(2,1)}), bf16[64,4,512]{2,1,0:T(4,128)(2,1)S(1)}, u32[]{:S(2)}, u32[]{:S(2)}) async-start(bf16[64,4,512]{2,1,0:T(4,128)(2,1)} %reshape.46), calls=%async_computation | async-start | bytes 524288 | tf_op jit(solution)/shard_map/rows_out/all_to_all | solution.py:222
  45.6 56.0 %collective-permute-start.2 = (bf16[4,640,256]{2,1,0:T(8,128)(2,1)S(1)}, bf16[4,640,256]{2,1,0:T(8,128)(2,1)}, u32[]{:S(2)}, u32[]{:S(2)}) collective-permute-start(bf16[4,640,256]{2,1,0:T(8,128)(2,1)S(1)} %all-to-all-done.3.mine_ref), channel_id=1, source_target_pairs={{0,1},{1,0},{2,3},{3,2},{4,5},{5,4},{6,7},{7,6},{8,9},{9,8},{10,11... | collective-permute-start | bytes 3932168 | tf_op jit(solution)/shard_map/pages_to_heads/ppermute | solution.py:231
  58.9 18.6 %all-to-all-start.1 = ((bf16[8,128,256]{2,1,0:T(8,128)(2,1)}), bf16[8,128,256]{2,1,0:T(8,128)(2,1)S(1)}, u32[]{:S(2)}, u32[]{:S(2)}) async-start(bf16[8,128,256]{2,1,0:T(8,128)(2,1)} %bitcast.5), calls=%async_computation.1 | async-start | bytes 1048576 | tf_op jit(solution)/shard_map/prefix_to_heads/all_to_all | solution.py:210
  67.2 19.0 %copy-start.3 = (s32[2,64]{1,0:T(2,128)S(1)}, s32[2,64]{1,0:T(2,128)}, u32[]{:S(2)}) copy-start(s32[2,64]{1,0:T(2,128)} %param.7) | copy-start | bytes 1540
  80.5 21.1 %all-to-all-start.2 = ((bf16[64,4,640]{2,1,0:T(4,128)(2,1)}), bf16[64,4,640]{2,1,0:T(4,128)(2,1)S(1)}, u32[]{:S(2)}, u32[]{:S(2)}) async-start(bf16[64,4,640]{2,1,0:T(4,128)(2,1)} %reshape.50), calls=%async_computation.2 | async-start | bytes 655360 | tf_op jit(solution)/shard_map/rows_back/all_to_all | solution.py:242

commit v2 on v1

v2 whole, which is shorter than its diff:
```python
import jax
import jax.numpy as jnp
from jax import lax
from jax.experimental import pallas as pl
from jax.experimental.pallas import tpu as pltpu
from jax.sharding import PartitionSpec as P

HQ = 32
KVH = 4
DH = 128
CAP = 2
STAT = 8
PRE = 128
PAGE_ROWS = 512
SCALE = DH ** (-0.5)
BF = jnp.bfloat16
F32 = jnp.float32
NT = (((1,), (1,)), ((), ()))
NN = (((1,), (0,)), ((), ()))
TN = (((0,), (0,)), ((), ()))
VMEM = pl.BlockSpec(memory_space=pltpu.VMEM)
SMEM = pl.BlockSpec(memory_space=pltpu.SMEM)
HBM = pl.BlockSpec(memory_space=pltpu.HBM)


def dot(a, b, dims):
    return lax.dot_general(a, b, dims, preferred_element_type=F32)


def call(kernel, outs, *operands, scratch=(), flops=0, nbytes=0, vmem=24, name=None):
    single = not isinstance(outs, tuple)
    specs = {"v": VMEM, "s": SMEM, "r": HBM}
    result = pl.pallas_call(
        kernel,
        out_shape=(outs,) if single else outs,
        in_specs=[specs[kind] for kind, _ in operands],
        out_specs=(VMEM,) if single else (VMEM,) * len(outs),
        scratch_shapes=list(scratch),
        compiler_params=pltpu.CompilerParams(vmem_limit_bytes=vmem << 20),
        cost_estimate=pl.CostEstimate(flops=flops, bytes_accessed=nbytes, transcendentals=0),
        name=name,
    )(*[array for _, array in operands])
    return result[0] if single else result


def split_kernel(seq_ref, pages_ref, prefix_ref, own_ref, *out_refs):
    chip = seq_ref[0] // 2
    core = lax.rem(seq_ref[0], 2)
    rows = own_ref.shape[0]
    for k, out_ref in enumerate(out_refs):
        target = lax.rem(chip + k, KVH)
        at = 0
        for ref in (pages_ref, prefix_ref):
            count = ref.shape[0]
            for part in range(2):
                cols = pl.ds(pl.multiple_of((part * KVH + target) * DH, DH), DH)
                out_ref[at : at + count, :] = ref[:, cols]
                at += count
        if k == 0:
            out_ref[at : at + rows, :] = own_ref[:, :DH]
            out_ref[at + rows :, :] = own_ref[:, 4 * DH :]
        else:
            chunk = jnp.minimum(2 - core + target, 4)
            out_ref[at:, :] = own_ref[:, pl.ds(pl.multiple_of(chunk * DH, DH), DH)]


def share_kernel(query_ref, *refs):
    out_ref = refs[-1]
    rows = query_ref.shape[0]
    at = 0
    for ref in refs[:-1]:
        out_ref[at : at + 2 * PRE, :] = ref[2 * PAGE_ROWS : 2 * PAGE_ROWS + 2 * PRE, :]
        at += 2 * PRE
    for h in range(query_ref.shape[1] // DH):
        out_ref[at : at + rows, :] = query_ref[:, h * DH : (h + 1) * DH]
        at += rows


def slot_of(route, rank, axis, rows):
    step = lax.broadcasted_iota(jnp.int32, route.shape, axis) >= rows // 2
    return route, step.astype(jnp.int32) * CAP + rank


def ranks(along, across, rows, axis):
    first = lax.broadcasted_iota(jnp.int32, (rows, rows), axis)
    second = lax.broadcasted_iota(jnp.int32, (rows, rows), 1 - axis)
    same = (along == across) & (first < second) & ((first < rows // 2) == (second < rows // 2))
    return jnp.sum(same.astype(jnp.int32), axis=axis, keepdims=True)


def route_both(route_ref):
    row = jnp.concatenate([route_ref[0:1, :], route_ref[1:2, :]], axis=1)
    rows = row.shape[1]
    column = jnp.broadcast_to(row, (rows, rows)).T[:, :1]
    return row, column


def slots_kernel(seq_ref, own_ref, near_ref, far_ref, route_ref, sent_ref, query_ref, line, wide):
    rows = own_ref.shape[0]
    width = own_ref.shape[1]
    heads = query_ref.shape[1] // DH
    count = sent_ref.shape[0] // heads
    line[:, :width] = far_ref[...]
    line[:, width : 2 * width] = near_ref[...]
    line[:, 2 * width :] = own_ref[...]
    first = pl.multiple_of((10 - seq_ref[0]) * DH, DH)
    query = line[:, pl.ds(first, query_ref.shape[1])]
    query_ref[...] = query
    row, column = route_both(route_ref)
    prompt, slot = slot_of(row, ranks(column, row, rows, 0), 1, rows)
    onehot = lax.broadcasted_iota(jnp.int32, (count, rows), 0) == prompt * (2 * CAP) + slot
    onehot = onehot.astype(F32).astype(BF)
    for h in range(heads):
        wide[pl.ds(h, count, stride=heads), :] = dot(onehot, query[:, h * DH : (h + 1) * DH], NN)
    sent_ref[...] = wide[...].astype(BF)


def thirds(value):
    high = value.astype(BF).astype(F32)
    rest = value - high
    middle = rest.astype(BF).astype(F32)
    low = (rest - middle).astype(BF).astype(F32)
    return [high, middle, low]


def prefix_kernel(query_ref, mine_ref, other_ref, out_ref):
    per_message = out_ref.shape[1] - STAT
    wide = 256
    blocks = [(ref, 2 * PRE * k) for ref in (mine_ref, other_ref) for k in range(KVH)]
    values_t = [ref[at + PRE : at + 2 * PRE, :].astype(F32).T.astype(BF) for ref, at in blocks]
    for c in range(query_ref.shape[0] // wide):
        query = query_ref[c * wide : (c + 1) * wide, :]
        tops, totals, parts = [], [], []
        for (ref, at), value_t in zip(blocks, values_t):
            scores = dot(ref[at : at + PRE, :], query, NT) * SCALE
            top = jnp.max(scores, axis=0, keepdims=True)
            weights = jnp.exp(scores - top).astype(BF)
            tops.append(top)
            totals.append(jnp.sum(weights.astype(F32), axis=0, keepdims=True))
            parts.append(dot(value_t, weights, NN))
        top = tops[0]
        for other in tops[1:]:
            top = jnp.maximum(top, other)
        total = jnp.zeros_like(top)
        mixed = jnp.zeros((DH, wide), F32)
        for block_top, block_total, block_part in zip(tops, totals, parts):
            factor = jnp.exp(block_top - top)
            total += block_total * factor
            mixed += block_part * factor
        mixed = (mixed / total).T.astype(BF)
        messages = wide // per_message
        at = c * messages
        out_ref[at : at + messages, :per_message, :] = mixed.reshape(messages, per_message, DH)
        zero = jnp.zeros_like(top)
        stats = jnp.concatenate(thirds(top) + thirds(total) + [zero, zero], axis=0).astype(BF)
        for g in range(wide // DH):
            for i in range(DH // per_message):
                out_ref[at + g * (DH // per_message) + i, per_message:, :] = stats[:, g * DH : (g + 1) * DH]


def page_kernel(seq_ref, mine_ref, other_ref, parent_ref, *refs):
    pieces, kept_ref, sent_ref = refs[:4], refs[4], refs[5]
    first = 2 * PRE * KVH
    half = mine_ref.shape[0] - first
    rows = 2 * parent_ref.shape[1]
    heads = half // rows
    count = PAGE_ROWS
    seg = 16
    tail = 2 * count + 2 * PRE
    query = jnp.concatenate([mine_ref[first:, :], other_ref[first:, :]], axis=0)
    parent = jnp.concatenate([parent_ref[0:1, :], parent_ref[1:2, :]] * (2 * heads), axis=1)
    scores = []
    for ref in pieces:
        every = dot(ref[:count, :], query, NT)
        held = every[:seg, :]
        for j in range(1, count // seg):
            held = jnp.where(parent == j, every[j * seg : (j + 1) * seg, :], held)
        scores.append(held * SCALE)
    top = jnp.max(scores[0], axis=0, keepdims=True)
    for held in scores[1:]:
        top = jnp.maximum(top, jnp.max(held, axis=0, keepdims=True))
    total = jnp.zeros_like(top)
    mixed = jnp.zeros((DH, 2 * half), F32)
    for ref, held in zip(pieces, scores):
        weights = jnp.exp(held - top).astype(BF).astype(F32)
        total += jnp.sum(weights, axis=0, keepdims=True)
        chosen = jnp.concatenate([jnp.where(parent == j, weights, 0.0) for j in range(count // seg)], axis=0)
        mixed += dot(ref[count : 2 * count, :], chosen.astype(BF), TN)
    chip = seq_ref[0] // 2
    own = jnp.where(chip == 0, pieces[1][tail:, :], jnp.where(chip == 1, pieces[2][tail:, :], pieces[3][tail:, :]))
    last = chip == 3
    key = jnp.where(last, pieces[0][tail : tail + rows, :], own).astype(F32).T
    value = jnp.where(last, pieces[0][tail + rows :, :], own).astype(F32).T
    query_t = query.astype(F32).T
    own_score = jnp.concatenate(
        [
            jnp.sum(query_t[:, h * rows : (h + 1) * rows] * key, axis=0, keepdims=True)
            for h in range(2 * heads)
        ],
        axis=1,
    )
    stats = jnp.concatenate([top, total, own_score * SCALE] + [jnp.zeros_like(top)] * 5, axis=0)
    for n, ref in enumerate((kept_ref, sent_ref)):
        ref[:DH, :half] = mixed[:, n * half : (n + 1) * half]
        ref[:DH, half:] = value
        ref[DH:, :half] = stats[:, n * half : (n + 1) * half]
        ref[DH:, half:] = jnp.zeros((STAT, DH), F32)


def merge_kernel(seq_ref, kept_ref, got_ref, out_ref, stat_ref):
    rows = out_ref.shape[0]
    heads = out_ref.shape[1] // DH
    half = heads * rows
    even = lax.rem(seq_ref[0], 2) == 0
    last = seq_ref[0] // 2 == 3
    has_key = even != last
    kept, got = kept_ref[DH:, :half], got_ref[DH:, :half]
    own_score = jnp.where(has_key, kept[2:3, :], got[2:3, :])
    best = jnp.maximum(jnp.maximum(kept[0:1, :], got[0:1, :]), own_score)
    factor_kept = jnp.exp(kept[0:1, :] - best)
    factor_got = jnp.exp(got[0:1, :] - best)
    factor_own = jnp.exp(own_score - best)
    total = kept[1:2, :] * factor_kept + got[1:2, :] * factor_got + factor_own
    value = jnp.where(even, got_ref[:DH, half:], kept_ref[:DH, half:])
    for h in range(heads):
        cols = slice(h * rows, (h + 1) * rows)
        part = kept_ref[:DH, cols] * factor_kept[:, cols] + got_ref[:DH, cols] * factor_got[:, cols]
        part += value * factor_own[:, cols]
        out_ref[:, h * DH : (h + 1) * DH] = part.T
    stats = [line[:, h * rows : (h + 1) * rows] for line in (best, total) for h in range(heads)]
    stats.append(jnp.zeros((DH - 2 * heads, rows), F32))
    stat_ref[...] = jnp.concatenate(stats, axis=0).T


def finish_kernel(prompt_ref, back_ref, route_ref, part_ref, stat_ref, out_ref, wide):
    rows = part_ref.shape[0]
    heads = part_ref.shape[1] // DH
    slots = 2 * CAP
    per_message = slots * heads
    stride = per_message + STAT
    messages = back_ref.shape[0] // stride
    wide[...] = back_ref[...].astype(F32)
    row, column = route_both(route_ref)
    prompt, slot = slot_of(column, ranks(row, column, rows, 1), 0, rows)
    lane = lax.broadcasted_iota(jnp.int32, (rows, slots * messages), 1)
    onehot = (lane == slot * messages + prompt).astype(F32).astype(BF)
    lane = lax.broadcasted_iota(jnp.int32, (rows, messages), 1)
    chosen = (lane == prompt).astype(F32).astype(BF)

    def line(at):
        return wide[pl.ds(at, messages, stride=stride), :].astype(BF)

    found = [dot(chosen, line(per_message + v), NN) for v in range(6)]
    tops = found[0] + found[1] + found[2]
    totals = found[3] + found[4] + found[5]
    group = lax.rem(prompt_ref[0], DH // per_message)
    lane = lax.broadcasted_iota(jnp.int32, (rows, DH), 1)
    stats = stat_ref[...]
    for h in range(heads):
        cols = slice(h * DH, (h + 1) * DH)
        lines = jnp.concatenate([line(s * heads + h) for s in range(slots)], axis=0)
        got = dot(onehot, lines, NN)
        mask = lane == group * per_message + slot * heads + h
        prefix_top = jnp.sum(jnp.where(mask, tops, 0.0), axis=1, keepdims=True)
        prefix_total = jnp.sum(jnp.where(mask, totals, 0.0), axis=1, keepdims=True)
        home_top = stats[:, h : h + 1]
        home_total = stats[:, heads + h : heads + h + 1]
        best = jnp.maximum(prefix_top, home_top)
        factor_prefix = jnp.exp(prefix_top - best) * prefix_total
        factor_home = jnp.exp(home_top - best)
        denom = factor_prefix + home_total * factor_home
        numer = got * factor_prefix + part_ref[:, cols] * factor_home
        out_ref[:, cols] = (numer / denom).astype(BF)


def body(beam_rows, route, parent, prefix_kv, pages):
    prompt_count = lax.axis_size("prompt")
    seq_count = lax.axis_size("seq")
    step_count, row_count, width = beam_rows.shape
    rows = step_count * row_count
    head_part = HQ // seq_count
    out_width = head_part * DH
    per_message = step_count * CAP * head_part
    slots = prompt_count * per_message
    seq_at = lax.axis_index("seq").astype(jnp.int32).reshape(1)
    prompt_at = lax.axis_index("prompt").astype(jnp.int32).reshape(1)
    own = beam_rows.reshape(rows, width)
    route = route.reshape(step_count, row_count)
    swap = [(i, i ^ 1) for i in range(seq_count)]

    def turn(value, k):
        return lax.ppermute(value, "seq", [(i, (i + 2 * k) % seq_count) for i in range(seq_count)])

    with jax.named_scope("rows_to_heads"):
        near = lax.ppermute(own, "seq", [(i, i + 1) for i in range(seq_count - 1)])
        far = lax.ppermute(own, "seq", [(4, 6), (5, 7)])
    with jax.named_scope("tokens_to_heads"):
        count = pages.shape[0] * pages.shape[1]
        pre = prefix_kv.shape[1]
        split = call(
            split_kernel,
            tuple(
                jax.ShapeDtypeStruct((2 * count + 2 * pre + (2 if k == 0 else 1) * rows, DH), BF) for k in range(4)
            ),
            ("s", seq_at), ("v", pages.reshape(count, pages.shape[2])), ("v", prefix_kv[0]), ("v", own),
            nbytes=3 << 20,
        )
        *split, near, far = lax.optimization_barrier((*split, near, far))
        pieces = [split[0]] + [turn(split[k], k) for k in range(1, 4)]
    with jax.named_scope("slots"):
        sent, query = call(
            slots_kernel,
            (jax.ShapeDtypeStruct((slots, DH), BF), jax.ShapeDtypeStruct((rows, out_width), BF)),
            ("s", seq_at), ("v", own), ("v", near), ("v", far), ("v", route),
            scratch=[pltpu.VMEM((rows, 3 * width), BF), pltpu.VMEM((slots, DH), F32)],
            flops=2 * slots * rows * DH,
            nbytes=1 << 20,
        )
    with jax.named_scope("rows_out"):
        sent = sent.reshape(prompt_count, per_message, DH)
        arrived = lax.all_to_all(sent, "prompt", 0, 0, tiled=True).reshape(slots, DH)
    with jax.named_scope("share_cores"):
        shared = call(
            share_kernel,
            jax.ShapeDtypeStruct((KVH * 2 * pre + rows * head_part, DH), BF),
            ("v", query), *[("v", piece) for piece in pieces],
            nbytes=1 << 20,
        )
        other = lax.ppermute(shared, "seq", swap)
    with jax.named_scope("prefix_part"):
        part = call(
            prefix_kernel,
            jax.ShapeDtypeStruct((prompt_count, per_message + STAT, DH), BF),
            ("v", arrived), ("v", shared), ("v", other),
            flops=4 * slots * 1024 * DH,
            nbytes=1 << 20,
        )
    with jax.named_scope("rows_back"):
        back = lax.all_to_all(part, "prompt", 0, 0, tiled=True).reshape(-1, DH)
    with jax.named_scope("page_part"):
        payload = jax.ShapeDtypeStruct((DH + STAT, rows * head_part + DH), F32)
        kept, lent = call(
            page_kernel,
            (payload, payload),
            ("s", seq_at), ("v", shared), ("v", other), ("v", parent), *[("v", piece) for piece in pieces],
            flops=4 * rows * head_part * 4096 * DH,
            nbytes=2 << 20,
        )
        got = lax.ppermute(lent, "seq", swap)
    with jax.named_scope("page_merge"):
        home = call(
            merge_kernel,
            (jax.ShapeDtypeStruct((rows, out_width), F32), jax.ShapeDtypeStruct((rows, DH), F32)),
            ("s", seq_at), ("v", kept), ("v", got),
            flops=1 << 20,
            nbytes=1 << 20,
        )
    with jax.named_scope("finish"):
        attended = call(
            finish_kernel,
            jax.ShapeDtypeStruct((rows, out_width), BF),
            ("s", prompt_at), ("v", back), ("v", route), *[("v", value) for value in home],
            scratch=[pltpu.VMEM((prompt_count * (per_message + STAT), DH), F32)],
            flops=2 * slots * rows * DH,
            nbytes=1 << 20,
        )
    return attended.reshape(step_count, row_count, out_width)


def solution(mesh):
    return jax.shard_map(
        body,
        mesh=mesh,
        in_specs=(
            P(None, "prompt", "seq"),
            P(None, "prompt", None),
            P(None, "prompt"),
            P("prompt", "seq", None),
            P("prompt", "seq", None),
        ),
        out_specs=P(None, "prompt", "seq"),
        check_vma=False,
    )
```

time: 120 us -> 78 us (0.65)
  waiting for transfers between devices: 50.3 us -> 21.4 us
  Pallas kernels: 20.5 us -> 8.61 us
  starting transfers between devices: 39 us -> 44.2 us
  local copies, waits for them, and re-layouts: 7.88 us -> 3.09 us
  other arithmetic: 1.84 us -> 0 us
    all_to_all x4 -> x2, waiting for transfers between devices: 50.3 us -> 19.8 us  [the longest x1 10.4 us: body(): lax.all_to_all(sent, 'prompt', 0, 0, tiled=True).reshape(slots, DH)]
    ppermute x1 -> x5, starting transfers between devices: 1.92 us -> 19.4 us  [the longest x3 15.5 us: turn(): lax.ppermute(value, 'seq', [(i, (i + 2 * k) % seq_count) for i in range(s...]
    all_to_all x4 -> x2, starting transfers between devices: 34.8 us -> 22.5 us  [the longest x1 16.5 us: body(): lax.all_to_all(sent, 'prompt', 0, 0, tiled=True).reshape(slots, DH)]
    pallas_call x4 -> x7, Pallas kernels: 20.5 us -> 8.61 us  [call(): pl.pallas_call(kernel, out_shape=(outs,) if single else outs, in_specs=[s...]
    reshape x11 -> x0, local copies, waits for them, and re-layouts: 5.48 us -> none  [the longest x4 3.46 us: by_head(): tokens.reshape(count, 2, KVH, DH).transpose(2, 0, 1, 3)]
    unnamed x10, local copies, waits for them, and re-layouts: 0.7 us -> 3.09 us
    ppermute x1 -> x5, waiting for transfers between devices: 0.01 us -> 1.63 us  [the longest x1 1.62 us: body(): got = lax.ppermute(lent, 'seq', swap)]
  transfers between devices with their start and end apart: 7 -> 9, of which waited for: 4 -> 3; matrix products, arithmetic and copies ran while one was open for 4% -> 0% of each run, Pallas kernels for 2% -> 5%
where the time goes in v2:
time: 78 us; the launch traced here: 77.5 us
  starting transfers between devices  44.2 us (57%)
  waiting for transfers between devices  21.4 us (27%)
  Pallas kernels  8.61 us (11%)
  local copies, waits for them, and re-layouts  3.09 us (4%)
    all_to_all x1, starting transfers between devices, body(): lax.all_to_all(sent, 'prompt', 0, 0, tiled=True).reshape(slots, DH)  16.5 us
    ppermute x3, starting transfers between devices, turn(): lax.ppermute(value, 'seq', [(i, (i + 2 * k) % seq_count) for i in range(s...  15.5 us
    all_to_all x1, waiting for transfers between devices, body(): lax.all_to_all(sent, 'prompt', 0, 0, tiled=True).reshape(slots, DH)  10.4 us
    all_to_all x1, waiting for transfers between devices, body(): back = lax.all_to_all(part, 'prompt', 0, 0, tiled=True).reshape(-1, DH)  9.4 us
    pallas_call x7, Pallas kernels, call(): pl.pallas_call(kernel, out_shape=(outs,) if single else outs, in_specs=[s...  8.61 us
    all_to_all x1, starting transfers between devices, body(): back = lax.all_to_all(part, 'prompt', 0, 0, tiled=True).reshape(-1, DH)  5.98 us
    unnamed x10, local copies, waits for them, and re-layouts  3.09 us
    ppermute x1, starting transfers between devices, body(): other = lax.ppermute(shared, 'seq', swap)  1.92 us
  transfers between devices with their start and end apart: 9, of which 3 were waited for; matrix products, arithmetic and copies ran while one was open for 0% of the time, Pallas kernels for 5%

profile of v2, /device:TPU:16, one launch (start us, length us, event | category | flops | bytes accessed | tf_op | source)
XLA Modules:
  0.0 77.5 jit_solution(6100210908744909607)
XLA Ops:
  0.0 0.7 collective-permute-start.1
  0.7 1.7 %collective-permute-start = (bf16[128,640]{1,0:T(8,128)(2,1)}, bf16[128,640]{1,0:T(8,128)(2,1)S(1)}, u32[]{:S(2)}, u32[]{:S(2)}) collective-permute-start(bf16[128,640]{1,0:T(8,128)(2,1)} %bitcast.13), channel_id=1, source_target_pairs={{0,1},{1,2},{2,3},{3,4},{4,5},{5,6},{6,7},{8,9},{9,10},{10,11},{11... | collective-permute-start | bytes 491528 | tf_op jit(solution)/shard_map/rows_to_heads/ppermute | solution.py:295
  2.4 1.2 %copy-done = bf16[32,16,1024]{2,1,0:T(8,128)(2,1)S(1)} copy-done((bf16[32,16,1024]{2,1,0:T(8,128)(2,1)S(1)}, bf16[32,16,1024]{2,1,0:T(8,128)(2,1)}, u32[]{:S(2)}) %copy-start) | copy-done | bytes 1048600
  3.7 0.9 %copy-done.1 = bf16[2,64,640]{2,1,0:T(8,128)(2,1)S(1)} copy-done((bf16[2,64,640]{2,1,0:T(8,128)(2,1)S(1)}, bf16[2,64,640]{2,1,0:T(8,128)(2,1)}, u32[]{:S(2)}) %copy-start.1) | copy-done | bytes 163864
  4.6 0.9 %copy-done.2 = bf16[1,128,1024]{2,1,0:T(8,128)(2,1)S(1)} copy-done((bf16[1,128,1024]{2,1,0:T(8,128)(2,1)S(1)}, bf16[1,128,1024]{2,1,0:T(8,128)(2,1)}, u32[]{:S(2)}) %copy-start.2) | copy-done | bytes 262168
  5.5 0.4 tokens_to_heads.1
  5.9 0.0 collective-permute-done.near_ref
  5.9 0.0 copy-start.3
  5.9 5.1 %collective-permute-start.2 = (bf16[1408,128]{1,0:T(8,128)(2,1)S(1)}, bf16[1408,128]{1,0:T(8,128)(2,1)S(1)}, u32[]{:S(2)}, u32[]{:S(2)}) collective-permute-start(bf16[1408,128]{1,0:T(8,128)(2,1)S(1)} %get-tuple-element.30), channel_id=1, source_target_pairs={{0,2},{1,3},{2,4},{3,5},{4,6},{5,7},{6,0},{7,1},{8,10},{9,11},{10,... | collective-permute-start | bytes 1081352 | tf_op jit(solution)/shard_map/tokens_to_heads/ppermute | solution.py:292
  11.0 6.9 %collective-permute-start.3 = (bf16[1408,128]{1,0:T(8,128)(2,1)S(1)}, bf16[1408,128]{1,0:T(8,128)(2,1)S(1)}, u32[]{:S(2)}, u32[]{:S(2)}) collective-permute-start(bf16[1408,128]{1,0:T(8,128)(2,1)S(1)} %get-tuple-element.31), channel_id=1, source_target_pairs={{0,4},{1,5},{2,6},{3,7},{4,0},{5,1},{6,2},{7,3},{8,12},{9,13},{10,... | collective-permute-start | bytes 1081352 | tf_op jit(solution)/shard_map/tokens_to_heads/ppermute | solution.py:292
  18.0 3.5 %collective-permute-start.4 = (bf16[1408,128]{1,0:T(8,128)(2,1)S(1)}, bf16[1408,128]{1,0:T(8,128)(2,1)S(1)}, u32[]{:S(2)}, u32[]{:S(2)}) collective-permute-start(bf16[1408,128]{1,0:T(8,128)(2,1)S(1)} %get-tuple-element.32), channel_id=1, source_target_pairs={{0,6},{1,7},{2,0},{3,1},{4,2},{5,3},{6,4},{7,5},{8,14},{9,15},{10,... | collective-permute-start | bytes 1081352 | tf_op jit(solution)/shard_map/tokens_to_heads/ppermute | solution.py:292
  21.5 1.2 %slots.1 = (bf16[1024,128]{1,0:T(8,128)(2,1)}, bf16[128,512]{1,0:T(8,128)(2,1)S(1)}) custom-call(s32[1]{0:T(128)} %bitcast.1.seq_ref, bf16[128,640]{1,0:T(8,128)(2,1)S(1)} %bitcast.15, bf16[128,640]{1,0:T(8,128)(2,1)S(1)} %collective-permute-done.near_ref, bf16[128,640]{1,0:T(8,128)(2,1)S(1)} %collective-permute-done.1.far_ref, s32[2,64]{1,0:T(2,128)S(1)} %bitcast.18), custom_call_target="tpu_custom_call" | custom-call | flops 33554432 | bytes 1048576 | tf_op jit(solution)/shard_map/slots/pallas_call | solution.py:33
  22.7 16.5 %all-to-all-start = ((bf16[64,16,128]{2,1,0:T(8,128)(2,1)}), bf16[64,16,128]{2,1,0:T(8,128)(2,1)S(1)}, u32[]{:S(2)}, u32[]{:S(2)}) async-start(bf16[64,16,128]{2,1,0:T(8,128)(2,1)} %bitcast.6), calls=%async_computation | async-start | bytes 524288 | tf_op jit(solution)/shard_map/rows_out/all_to_all | solution.py:321
  39.1 0.0 collective-permute-done.2.refs_1_
  39.2 1.9 %collective-permute-start.5 = (bf16[1536,128]{1,0:T(8,128)(2,1)S(1)}, bf16[1536,128]{1,0:T(8,128)(2,1)S(1)}, u32[]{:S(2)}, u32[]{:S(2)}) collective-permute-start(bf16[1536,128]{1,0:T(8,128)(2,1)S(1)} %share_cores.1.mine_ref), channel_id=1, source_target_pairs={{0,1},{1,0},{2,3},{3,2},{4,5},{5,4},{6,7},{7,6},{8,9},{9,8},{10,11... | collective-permute-start | bytes 1179656 | tf_op jit(solution)/shard_map/share_cores/ppermute | solution.py:329
  41.2 10.4 %all-to-all-done = bf16[64,16,128]{2,1,0:T(8,128)(2,1)S(1)} async-done(((bf16[64,16,128]{2,1,0:T(8,128)(2,1)}), bf16[64,16,128]{2,1,0:T(8,128)(2,1)S(1)}, u32[]{:S(2)}, u32[]{:S(2)}) %all-to-all-start) | async-done | bytes 262176 | tf_op jit(solution)/shard_map/rows_out/all_to_all | solution.py:321
  51.5 3.0 %prefix_part.1 = bf16[64,24,128]{2,1,0:T(8,128)(2,1)} custom-call(bf16[1024,128]{1,0:T(8,128)(2,1)S(1)} %bitcast.16, bf16[1536,128]{1,0:T(8,128)(2,1)S(1)} %share_cores.1.mine_ref, bf16[1536,128]{1,0:T(8,128)(2,1)S(1)} %collective-permute-done.5.other_ref), custom_call_target="tpu_custom_call" | custom-call | flops 536870912 | bytes 1048576 | tf_op jit(solution)/shard_map/prefix_part/pallas_call | solution.py:33
  54.5 6.0 %all-to-all-start.1 = ((bf16[64,24,128]{2,1,0:T(8,128)(2,1)}), bf16[64,24,128]{2,1,0:T(8,128)(2,1)S(1)}, u32[]{:S(2)}, u32[]{:S(2)}) async-start(bf16[64,24,128]{2,1,0:T(8,128)(2,1)} %prefix_part.1), calls=%async_computation.1 | async-start | bytes 786432 | tf_op jit(solution)/shard_map/rows_back/all_to_all | solution.py:339
  60.6 2.0 %page_part.1 = (f32[136,640]{1,0:T(8,128)S(1)}, f32[136,640]{1,0:T(8,128)S(1)}) custom-call(s32[1]{0:T(128)} %bitcast.1.seq_ref, bf16[1536,128]{1,0:T(8,128)(2,1)S(1)} %share_cores.1.mine_ref, bf16[1536,128]{1,0:T(8,128)(2,1)S(1)} %collective-permute-done.5.other_ref, s32[2,64]{1,0:T(2,128)S(1)} %copy-done.4, ...), custom_call_target="tpu_custom_call" | custom-call | flops 1073741824 | bytes 2097152 | tf_op jit(solution)/shard_map/page_part/pallas_call | solution.py:33
  62.5 1.9 %collective-permute-start.6 = (f32[136,640]{1,0:T(8,128)S(1)}, f32[136,640]{1,0:T(8,128)S(1)}, u32[]{:S(2)}, u32[]{:S(2)}) collective-permute-start(f32[136,640]{1,0:T(8,128)S(1)} %get-tuple-element.34), channel_id=1, source_target_pairs={{0,1},{1,0},{2,3},{3,2},{4,5},{5,4},{6,7},{7,6},{8,9},{9,8},{10,11... | collective-permute-start | bytes 1044488 | tf_op jit(solution)/shard_map/page_part/ppermute | solution.py:349
  64.5 1.6 %collective-permute-done.6.got_ref = f32[136,640]{1,0:T(8,128)S(1)} collective-permute-done((f32[136,640]{1,0:T(8,128)S(1)}, f32[136,640]{1,0:T(8,128)S(1)}, u32[]{:S(2)}, u32[]{:S(2)}) %collective-permute-start.6) | collective-permute-done | bytes 348192 | tf_op jit(solution)/shard_map/page_part/ppermute | solution.py:349
  66.1 0.2 page_merge.1
  66.3 9.4 %all-to-all-done.1 = bf16[64,24,128]{2,1,0:T(8,128)(2,1)S(1)} async-done(((bf16[64,24,128]{2,1,0:T(8,128)(2,1)}), bf16[64,24,128]{2,1,0:T(8,128)(2,1)S(1)}, u32[]{:S(2)}, u32[]{:S(2)}) %all-to-all-start.1) | async-done | bytes 393248 | tf_op jit(solution)/shard_map/rows_back/all_to_all | solution.py:339
  75.7 1.9 %finish.1 = bf16[128,512]{1,0:T(8,128)(2,1)} custom-call(s32[1]{0:T(128)} %bitcast.prompt_ref, bf16[1536,128]{1,0:T(8,128)(2,1)S(1)} %bitcast.10, s32[2,64]{1,0:T(2,128)S(1)} %bitcast.19, f32[128,512]{1,0:T(8,128)S(1)} %get-tuple-element.35.part_ref, f32[128,128]{1,0:T(8,128)S(1)} %get-tuple-element.36.stat_ref), custom_call_target="tpu_custom_call" | custom-call | flops 33554432 | bytes 1048576 | tf_op jit(solution)/shard_map/finish/pallas_call | solution.py:33
  (11 shorter events, 0.1 us)
Async XLA Ops:
  0.0 5.9 %collective-permute-start.1 = (bf16[128,640]{1,0:T(8,128)(2,1)}, bf16[128,640]{1,0:T(8,128)(2,1)S(1)}, u32[]{:S(2)}, u32[]{:S(2)}) collective-permute-start(bf16[128,640]{1,0:T(8,128)(2,1)} %bitcast.12), channel_id=1, source_target_pairs={{4,6},{5,7},{12,14},{13,15},{20,22},{21,23},{28,30},{29,31},{36,38... | collective-permute-start | bytes 491528 | tf_op jit(solution)/shard_map/rows_to_heads/ppermute | solution.py:296
  0.7 5.2 %collective-permute-start = (bf16[128,640]{1,0:T(8,128)(2,1)}, bf16[128,640]{1,0:T(8,128)(2,1)S(1)}, u32[]{:S(2)}, u32[]{:S(2)}) collective-permute-start(bf16[128,640]{1,0:T(8,128)(2,1)} %bitcast.13), channel_id=1, source_target_pairs={{0,1},{1,2},{2,3},{3,4},{4,5},{5,6},{6,7},{8,9},{9,10},{10,11},{11... | collective-permute-start | bytes 491528 | tf_op jit(solution)/shard_map/rows_to_heads/ppermute | solution.py:295
  2.4 1.2 %copy-start = (bf16[32,16,1024]{2,1,0:T(8,128)(2,1)S(1)}, bf16[32,16,1024]{2,1,0:T(8,128)(2,1)}, u32[]{:S(2)}) copy-start(bf16[32,16,1024]{2,1,0:T(8,128)(2,1)} %param.9) | copy-start | bytes 3145732
  3.7 0.9 %copy-start.1 = (bf16[2,64,640]{2,1,0:T(8,128)(2,1)S(1)}, bf16[2,64,640]{2,1,0:T(8,128)(2,1)}, u32[]{:S(2)}) copy-start(bf16[2,64,640]{2,1,0:T(8,128)(2,1)} %param.5) | copy-start | bytes 491524
  4.6 0.9 %copy-start.2 = (bf16[1,128,1024]{2,1,0:T(8,128)(2,1)S(1)}, bf16[1,128,1024]{2,1,0:T(8,128)(2,1)}, u32[]{:S(2)}) copy-start(bf16[1,128,1024]{2,1,0:T(8,128)(2,1)} %param.8) | copy-start | bytes 786436
  5.9 15.6 %copy-start.3 = (s32[2,64,1]{1,2,0:T(1,128)S(1)}, s32[2,64,1]{1,2,0:T(1,128)}, u32[]{:S(2)}) copy-start(s32[2,64,1]{1,2,0:T(1,128)} %param.6) | copy-start | bytes 1540
  5.9 33.2 %collective-permute-start.2 = (bf16[1408,128]{1,0:T(8,128)(2,1)S(1)}, bf16[1408,128]{1,0:T(8,128)(2,1)S(1)}, u32[]{:S(2)}, u32[]{:S(2)}) collective-permute-start(bf16[1408,128]{1,0:T(8,128)(2,1)S(1)} %get-tuple-element.30), channel_id=1, source_target_pairs={{0,2},{1,3},{2,4},{3,5},{4,6},{5,7},{6,0},{7,1},{8,10},{9,11},{10,... | collective-permute-start | bytes 1081352 | tf_op jit(solution)/shard_map/tokens_to_heads/ppermute | solution.py:292
  11.0 28.1 %collective-permute-start.3 = (bf16[1408,128]{1,0:T(8,128)(2,1)S(1)}, bf16[1408,128]{1,0:T(8,128)(2,1)S(1)}, u32[]{:S(2)}, u32[]{:S(2)}) collective-permute-start(bf16[1408,128]{1,0:T(8,128)(2,1)S(1)} %get-tuple-element.31), channel_id=1, source_target_pairs={{0,4},{1,5},{2,6},{3,7},{4,0},{5,1},{6,2},{7,3},{8,12},{9,13},{10,... | collective-permute-start | bytes 1081352 | tf_op jit(solution)/shard_map/tokens_to_heads/ppermute | solution.py:292
  18.0 21.2 %collective-permute-start.4 = (bf16[1408,128]{1,0:T(8,128)(2,1)S(1)}, bf16[1408,128]{1,0:T(8,128)(2,1)S(1)}, u32[]{:S(2)}, u32[]{:S(2)}) collective-permute-start(bf16[1408,128]{1,0:T(8,128)(2,1)S(1)} %get-tuple-element.32), channel_id=1, source_target_pairs={{0,6},{1,7},{2,0},{3,1},{4,2},{5,3},{6,4},{7,5},{8,14},{9,15},{10,... | collective-permute-start | bytes 1081352 | tf_op jit(solution)/shard_map/tokens_to_heads/ppermute | solution.py:292
  22.7 28.9 %all-to-all-start = ((bf16[64,16,128]{2,1,0:T(8,128)(2,1)}), bf16[64,16,128]{2,1,0:T(8,128)(2,1)S(1)}, u32[]{:S(2)}, u32[]{:S(2)}) async-start(bf16[64,16,128]{2,1,0:T(8,128)(2,1)} %bitcast.6), calls=%async_computation | async-start | bytes 524288 | tf_op jit(solution)/shard_map/rows_out/all_to_all | solution.py:321
  39.2 12.3 %collective-permute-start.5 = (bf16[1536,128]{1,0:T(8,128)(2,1)S(1)}, bf16[1536,128]{1,0:T(8,128)(2,1)S(1)}, u32[]{:S(2)}, u32[]{:S(2)}) collective-permute-start(bf16[1536,128]{1,0:T(8,128)(2,1)S(1)} %share_cores.1.mine_ref), channel_id=1, source_target_pairs={{0,1},{1,0},{2,3},{3,2},{4,5},{5,4},{6,7},{7,6},{8,9},{9,8},{10,11... | collective-permute-start | bytes 1179656 | tf_op jit(solution)/shard_map/share_cores/ppermute | solution.py:329
  54.5 6.0 %copy-start.4 = (s32[2,64]{1,0:T(2,128)S(1)}, s32[2,64]{1,0:T(2,128)}, u32[]{:S(2)}) copy-start(s32[2,64]{1,0:T(2,128)} %parent_ref.1) | copy-start | bytes 1540
  54.5 21.1 %all-to-all-start.1 = ((bf16[64,24,128]{2,1,0:T(8,128)(2,1)}), bf16[64,24,128]{2,1,0:T(8,128)(2,1)S(1)}, u32[]{:S(2)}, u32[]{:S(2)}) async-start(bf16[64,24,128]{2,1,0:T(8,128)(2,1)} %prefix_part.1), calls=%async_computation.1 | async-start | bytes 786432 | tf_op jit(solution)/shard_map/rows_back/all_to_all | solution.py:339
  62.5 3.6 %collective-permute-start.6 = (f32[136,640]{1,0:T(8,128)S(1)}, f32[136,640]{1,0:T(8,128)S(1)}, u32[]{:S(2)}, u32[]{:S(2)}) collective-permute-start(f32[136,640]{1,0:T(8,128)S(1)} %get-tuple-element.34), channel_id=1, source_target_pairs={{0,1},{1,0},{2,3},{3,2},{4,5},{5,4},{6,7},{7,6},{8,9},{9,8},{10,11... | collective-permute-start | bytes 1044488 | tf_op jit(solution)/shard_map/page_part/ppermute | solution.py:349

commit v3 on v2

--- a/solution.py
+++ b/solution.py
@@ -9,10 +9,13 @@
 KVH = 4
 DH = 128
 CAP = 2
-STAT = 8
+STAT = 2
+ROWSTAT = 8
+MESSAGE = 16 + STAT
 PRE = 128
 PAGE_ROWS = 512
 SCALE = DH ** (-0.5)
+LOG2E = 1.4426950408889634
 BF = jnp.bfloat16
 F32 = jnp.float32
 NT = (((1,), (1,)), ((), ()))
@@ -27,14 +30,14 @@
     return lax.dot_general(a, b, dims, preferred_element_type=F32)
 
 
-def call(kernel, outs, *operands, scratch=(), flops=0, nbytes=0, vmem=24, name=None):
+def call(kernel, outs, *operands, scratch=(), flops=0, nbytes=0, vmem=24, out="v", name=None):
     single = not isinstance(outs, tuple)
     specs = {"v": VMEM, "s": SMEM, "r": HBM}
     result = pl.pallas_call(
         kernel,
         out_shape=(outs,) if single else outs,
         in_specs=[specs[kind] for kind, _ in operands],
-        out_specs=(VMEM,) if single else (VMEM,) * len(outs),
+        out_specs=(specs[out],) * (1 if single else len(outs)),
         scratch_shapes=list(scratch),
         compiler_params=pltpu.CompilerParams(vmem_limit_bytes=vmem << 20),
         cost_estimate=pl.CostEstimate(flops=flops, bytes_accessed=nbytes, transcendentals=0),
@@ -43,25 +46,44 @@
     return result[0] if single else result
 
 
-def split_kernel(seq_ref, pages_ref, prefix_ref, own_ref, *out_refs):
+def split_kernel(seq_ref, pages_ref, prefix_ref, own_ref, *refs):
+    count = len(refs) // 2
+    out_refs, held, sems = refs[:count], refs[count:-1], refs[-1]
     chip = seq_ref[0] // 2
     core = lax.rem(seq_ref[0], 2)
-    rows = own_ref.shape[0]
-    for k, out_ref in enumerate(out_refs):
+    order = (1, 3, 2, 0)
+    fetched = {}
+    used = count
+    for k in order:
         target = lax.rem(chip + k, KVH)
-        at = 0
-        for ref in (pages_ref, prefix_ref):
-            count = ref.shape[0]
-            for part in range(2):
-                cols = pl.ds(pl.multiple_of((part * KVH + target) * DH, DH), DH)
-                out_ref[at : at + count, :] = ref[:, cols]
-                at += count
+        pieces = [
+            (ref, pl.ds(pl.multiple_of((part * KVH + target) * DH, DH), DH))
+            for ref in (pages_ref, prefix_ref)
+            for part in range(2)
+        ]
         if k == 0:
-            out_ref[at : at + rows, :] = own_ref[:, :DH]
-            out_ref[at + rows :, :] = own_ref[:, 4 * DH :]
+            pieces += [(own_ref, pl.ds(0, DH)), (own_ref, pl.ds(4 * DH, DH))]
         else:
             chunk = jnp.minimum(2 - core + target, 4)
-            out_ref[at:, :] = own_ref[:, pl.ds(pl.multiple_of(chunk * DH, DH), DH)]
+            pieces.append((own_ref, pl.ds(pl.multiple_of(chunk * DH, DH), DH)))
+        at, fetched[k] = 0, []
+        for source, cols in pieces:
+            size = source.shape[0]
+            fetched[k].append(
+                pltpu.make_async_copy(source.at[:, cols], held[k].at[at : at + size, :], sems.at[used])
+            )
+            at += size
+            used += 1
+    for k in order:
+        for copy in fetched[k]:
+            copy.start()
+    written = [pltpu.make_async_copy(held[k], out_refs[k], sems.at[k]) for k in range(count)]
+    for k in order:
+        for copy in fetched[k]:
+            copy.wait()
+        written[k].start()
+    for copy in written:
+        copy.wait()
 
 
 def share_kernel(query_ref, *refs):
@@ -100,7 +122,7 @@
     width = own_ref.shape[1]
     heads = query_ref.shape[1] // DH
     count = sent_ref.shape[0] // heads
-    line[:, :width] = far_ref[...]
+    line[:, 3 * DH : width] = far_ref[...]
     line[:, width : 2 * width] = near_ref[...]
     line[:, 2 * width :] = own_ref[...]
     first = pl.multiple_of((10 - seq_ref[0]) * DH, DH)
@@ -123,8 +145,10 @@
     return [high, middle, low]
 
 
-def prefix_kernel(query_ref, mine_ref, other_ref, out_ref):
-    per_message = out_ref.shape[1] - STAT
+def prefix_kernel(query_ref, mine_ref, other_ref, out_ref, held):
+    messages = out_ref.shape[0] // MESSAGE
+    per_message = MESSAGE - STAT
+    stats = []
     wide = 256
     blocks = [(ref, 2 * PRE * k) for ref in (mine_ref, other_ref) for k in range(KVH)]
     values_t = [ref[at + PRE : at + 2 * PRE, :].astype(F32).T.astype(BF) for ref, at in blocks]
@@ -132,9 +156,9 @@
         query = query_ref[c * wide : (c + 1) * wide, :]
         tops, totals, parts = [], [], []
         for (ref, at), value_t in zip(blocks, values_t):
-            scores = dot(ref[at : at + PRE, :], query, NT) * SCALE
+            scores = dot(ref[at : at + PRE, :], query, NT)
             top = jnp.max(scores, axis=0, keepdims=True)
-            weights = jnp.exp(scores - top).astype(BF)
+            weights = jnp.exp2((scores - top) * (SCALE * LOG2E)).astype(BF)
             tops.append(top)
             totals.append(jnp.sum(weights.astype(F32), axis=0, keepdims=True))
             parts.append(dot(value_t, weights, NN))
@@ -144,18 +168,37 @@
         total = jnp.zeros_like(top)
         mixed = jnp.zeros((DH, wide), F32)
         for block_top, block_total, block_part in zip(tops, totals, parts):
-            factor = jnp.exp(block_top - top)
+            factor = jnp.exp2((block_top - top) * (SCALE * LOG2E))
             total += block_total * factor
             mixed += block_part * factor
-        mixed = (mixed / total).T.astype(BF)
-        messages = wide // per_message
-        at = c * messages
-        out_ref[at : at + messages, :per_message, :] = mixed.reshape(messages, per_message, DH)
-        zero = jnp.zeros_like(top)
-        stats = jnp.concatenate(thirds(top) + thirds(total) + [zero, zero], axis=0).astype(BF)
-        for g in range(wide // DH):
-            for i in range(DH // per_message):
-                out_ref[at + g * (DH // per_message) + i, per_message:, :] = stats[:, g * DH : (g + 1) * DH]
+        top = top * SCALE
+        mixed = (mixed * (1.0 / total)).T
+        for i in range(wide // per_message):
+            at = (c * wide // per_message + i) * MESSAGE
+            held[at : at + per_message, :] = mixed[i * per_message : (i + 1) * per_message, :]
+        stats += [jnp.concatenate(thirds(top) + thirds(total), axis=0)]
+    stats = jnp.concatenate(stats, axis=1)
+    terms = stats.shape[0]
+    near_by = DH // per_message
+    line = lax.broadcasted_iota(jnp.int32, (near_by, DH), 0)
+    lane = lax.broadcasted_iota(jnp.int32, (near_by, DH), 1)
+    mine = lane // per_message == line
+    spread = jnp.concatenate(
+        [
+            jnp.concatenate(
+                [jnp.where(mine, stats[v : v + 1, g * DH : (g + 1) * DH], 0.0) for v in range(terms)], axis=1
+            )
+            for g in range(messages // near_by)
+        ],
+        axis=0,
+    ).astype(BF)
+    source = lax.broadcasted_iota(jnp.int32, (terms * DH, DH), 0)
+    target = lax.broadcasted_iota(jnp.int32, (terms * DH, DH), 1)
+    place = (source // DH) * per_message + source % per_message
+    held_stats = dot(spread, (place == target).astype(F32).astype(BF), NN)
+    held[pl.ds(per_message, messages, stride=MESSAGE), :] = held_stats
+    held[pl.ds(per_message + 1, messages, stride=MESSAGE), :] = jnp.zeros((messages, DH), F32)
+    out_ref[...] = held[...].astype(BF)
 
 
 def page_kernel(seq_ref, mine_ref, other_ref, parent_ref, *refs):
@@ -204,10 +247,10 @@
         ref[:DH, :half] = mixed[:, n * half : (n + 1) * half]
         ref[:DH, half:] = value
         ref[DH:, :half] = stats[:, n * half : (n + 1) * half]
-        ref[DH:, half:] = jnp.zeros((STAT, DH), F32)
-
-
-def merge_kernel(seq_ref, kept_ref, got_ref, out_ref, stat_ref):
+        ref[DH:, half:] = jnp.zeros((ROWSTAT, DH), F32)
+
+
+def merge_kernel(seq_ref, kept_ref, got_ref, route_ref, out_ref, stat_ref, pick_ref, mask_ref):
     rows = out_ref.shape[0]
     heads = out_ref.shape[1] // DH
     half = heads * rows
@@ -230,47 +273,52 @@
     stats = [line[:, h * rows : (h + 1) * rows] for line in (best, total) for h in range(heads)]
     stats.append(jnp.zeros((DH - 2 * heads, rows), F32))
     stat_ref[...] = jnp.concatenate(stats, axis=0).T
-
-
-def finish_kernel(prompt_ref, back_ref, route_ref, part_ref, stat_ref, out_ref, wide):
-    rows = part_ref.shape[0]
+    slots = 2 * CAP
+    messages = pick_ref.shape[1] // (slots + 1)
+    row, column = route_both(route_ref)
+    prompt, slot = slot_of(column, ranks(row, column, rows, 1), 0, rows)
+    lane = lax.broadcasted_iota(jnp.int32, (rows, slots * messages), 1)
+    pick_ref[:, : slots * messages] = (lane == slot * messages + prompt).astype(F32).astype(BF)
+    lane = lax.broadcasted_iota(jnp.int32, (rows, messages), 1)
+    pick_ref[:, slots * messages :] = (lane == prompt).astype(F32).astype(BF)
+    lane = lax.broadcasted_iota(jnp.int32, (rows, DH), 1)
+    for h in range(heads):
+        mask_ref[:, h * DH : (h + 1) * DH] = (lane % (slots * heads) == slot * heads + h).astype(F32)
+
+
+def finish_kernel(back_ref, part_ref, stat_ref, pick_ref, mask_ref, out_ref, wide):
     heads = part_ref.shape[1] // DH
     slots = 2 * CAP
     per_message = slots * heads
-    stride = per_message + STAT
+    stride = MESSAGE
     messages = back_ref.shape[0] // stride
     wide[...] = back_ref[...].astype(F32)
-    row, column = route_both(route_ref)
-    prompt, slot = slot_of(column, ranks(row, column, rows, 1), 0, rows)
-    lane = lax.broadcasted_iota(jnp.int32, (rows, slots * messages), 1)
-    onehot = (lane == slot * messages + prompt).astype(F32).astype(BF)
-    lane = lax.broadcasted_iota(jnp.int32, (rows, messages), 1)
-    chosen = (lane == prompt).astype(F32).astype(BF)
+    onehot = pick_ref[:, : slots * messages]
+    chosen = pick_ref[:, slots * messages :]
 
     def line(at):
         return wide[pl.ds(at, messages, stride=stride), :].astype(BF)
 
-    found = [dot(chosen, line(per_message + v), NN) for v in range(6)]
-    tops = found[0] + found[1] + found[2]
-    totals = found[3] + found[4] + found[5]
-    group = lax.rem(prompt_ref[0], DH // per_message)
-    lane = lax.broadcasted_iota(jnp.int32, (rows, DH), 1)
+    found = dot(chosen, line(per_message), NN)
+    lane = lax.broadcasted_iota(jnp.int32, found.shape, 1)
+    tops = jnp.where(lane < 3 * per_message, found, 0.0)
+    totals = found - tops
     stats = stat_ref[...]
     for h in range(heads):
         cols = slice(h * DH, (h + 1) * DH)
         lines = jnp.concatenate([line(s * heads + h) for s in range(slots)], axis=0)
         got = dot(onehot, lines, NN)
-        mask = lane == group * per_message + slot * heads + h
-        prefix_top = jnp.sum(jnp.where(mask, tops, 0.0), axis=1, keepdims=True)
-        prefix_total = jnp.sum(jnp.where(mask, totals, 0.0), axis=1, keepdims=True)
+        mask = mask_ref[:, cols]
+        prefix_top = jnp.sum(tops * mask, axis=1, keepdims=True)
+        prefix_total = jnp.sum(totals * mask, axis=1, keepdims=True)
         home_top = stats[:, h : h + 1]
         home_total = stats[:, heads + h : heads + h + 1]
         best = jnp.maximum(prefix_top, home_top)
         factor_prefix = jnp.exp(prefix_top - best) * prefix_total
         factor_home = jnp.exp(home_top - best)
-        denom = factor_prefix + home_total * factor_home
-        numer = got * factor_prefix + part_ref[:, cols] * factor_home
-        out_ref[:, cols] = (numer / denom).astype(BF)
+        scale = 1.0 / (factor_prefix + home_total * factor_home)
+        mixed = got * (factor_prefix * scale) + part_ref[:, cols] * (factor_home * scale)
+        out_ref[:, cols] = mixed.astype(BF)
 
 
 def body(beam_rows, route, parent, prefix_kv, pages):
@@ -283,7 +331,6 @@
     per_message = step_count * CAP * head_part
     slots = prompt_count * per_message
     seq_at = lax.axis_index("seq").astype(jnp.int32).reshape(1)
-    prompt_at = lax.axis_index("prompt").astype(jnp.int32).reshape(1)
     own = beam_rows.reshape(rows, width)
     route = route.reshape(step_count, row_count)
     swap = [(i, i ^ 1) for i in range(seq_count)]
@@ -293,7 +340,7 @@
 
     with jax.named_scope("rows_to_heads"):
         near = lax.ppermute(own, "seq", [(i, i + 1) for i in range(seq_count - 1)])
-        far = lax.ppermute(own, "seq", [(4, 6), (5, 7)])
+        far = lax.ppermute(own[:, 3 * DH :], "seq", [(4, 6), (5, 7)])
     with jax.named_scope("tokens_to_heads"):
         count = pages.shape[0] * pages.shape[1]
         pre = prefix_kv.shape[1]
@@ -302,8 +349,13 @@
             tuple(
                 jax.ShapeDtypeStruct((2 * count + 2 * pre + (2 if k == 0 else 1) * rows, DH), BF) for k in range(4)
             ),
-            ("s", seq_at), ("v", pages.reshape(count, pages.shape[2])), ("v", prefix_kv[0]), ("v", own),
+            ("s", seq_at), ("r", pages.reshape(count, pages.shape[2])), ("r", prefix_kv[0]), ("r", own),
+            scratch=[
+                pltpu.VMEM((2 * count + 2 * pre + (2 if k == 0 else 1) * rows, DH), BF) for k in range(4)
+            ] + [pltpu.SemaphoreType.DMA((25,))],
             nbytes=3 << 20,
+            vmem=58,
+            out="r",
         )
         *split, near, far = lax.optimization_barrier((*split, near, far))
         pieces = [split[0]] + [turn(split[k], k) for k in range(1, 4)]
@@ -330,15 +382,17 @@
     with jax.named_scope("prefix_part"):
         part = call(
             prefix_kernel,
-            jax.ShapeDtypeStruct((prompt_count, per_message + STAT, DH), BF),
+            jax.ShapeDtypeStruct((prompt_count * MESSAGE, DH), BF),
             ("v", arrived), ("v", shared), ("v", other),
+            scratch=[pltpu.VMEM((prompt_count * MESSAGE, DH), F32)],
             flops=4 * slots * 1024 * DH,
             nbytes=1 << 20,
         )
     with jax.named_scope("rows_back"):
+        part = part.reshape(prompt_count, MESSAGE // 2, 2, DH)
         back = lax.all_to_all(part, "prompt", 0, 0, tiled=True).reshape(-1, DH)
     with jax.named_scope("page_part"):
-        payload = jax.ShapeDtypeStruct((DH + STAT, rows * head_part + DH), F32)
+        payload = jax.ShapeDtypeStruct((DH + ROWSTAT, rows * head_part + DH), F32)
         kept, lent = call(
             page_kernel,
             (payload, payload),
@@ -348,10 +402,15 @@
         )
         got = lax.ppermute(lent, "seq", swap)
     with jax.named_scope("page_merge"):
-        home = call(
+        merged = call(
             merge_kernel,
-            (jax.ShapeDtypeStruct((rows, out_width), F32), jax.ShapeDtypeStruct((rows, DH), F32)),
-            ("s", seq_at), ("v", kept), ("v", got),
+            (
+                jax.ShapeDtypeStruct((rows, out_width), F32),
+                jax.ShapeDtypeStruct((rows, DH), F32),
+                jax.ShapeDtypeStruct((rows, (step_count * CAP + 1) * prompt_count), BF),
+                jax.ShapeDtypeStruct((rows, out_width), F32),
+            ),
+            ("s", seq_at), ("v", kept), ("v", got), ("v", route),
             flops=1 << 20,
             nbytes=1 << 20,
         )
@@ -359,8 +418,8 @@
         attended = call(
             finish_kernel,
             jax.ShapeDtypeStruct((rows, out_width), BF),
-            ("s", prompt_at), ("v", back), ("v", route), *[("v", value) for value in home],
-            scratch=[pltpu.VMEM((prompt_count * (per_message + STAT), DH), F32)],
+            ("v", back), *[("v", value) for value in merged],
+            scratch=[pltpu.VMEM((prompt_count * MESSAGE, DH), F32)],
             flops=2 * slots * rows * DH,
             nbytes=1 << 20,
         )

time: 78 us -> 74.6 us (0.956)
  the two profiles are of different devices: /device:TPU:16 before, /device:TPU:2 now
where the time goes in v3:
time: 74.6 us; the launch traced here: 74.2 us
  starting transfers between devices  40.4 us (54%)
  waiting for transfers between devices  22.2 us (30%)
  Pallas kernels  10.4 us (14%)
  local copies, waits for them, and re-layouts  0.87 us (1%)
    all_to_all x1, starting transfers between devices, body(): lax.all_to_all(sent, 'prompt', 0, 0, tiled=True).reshape(slots, DH)  16.6 us
    ppermute x3, starting transfers between devices, turn(): lax.ppermute(value, 'seq', [(i, (i + 2 * k) % seq_count) for i in range(s...  12.7 us
    all_to_all x1, waiting for transfers between devices, body(): lax.all_to_all(sent, 'prompt', 0, 0, tiled=True).reshape(slots, DH)  11.5 us
    pallas_call x7, Pallas kernels, call(): pl.pallas_call(kernel, out_shape=(outs,) if single else outs, in_specs=[s...  10.4 us
    all_to_all x1, waiting for transfers between devices, body(): back = lax.all_to_all(part, 'prompt', 0, 0, tiled=True).reshape(-1, DH)  8.16 us
    all_to_all x1, starting transfers between devices, body(): back = lax.all_to_all(part, 'prompt', 0, 0, tiled=True).reshape(-1, DH)  4.76 us
    ppermute x1, starting transfers between devices, body(): other = lax.ppermute(shared, 'seq', swap)  1.92 us
    ppermute x1, starting transfers between devices, body(): got = lax.ppermute(lent, 'seq', swap)  1.92 us
  transfers between devices with their start and end apart: 9, of which 4 were waited for; matrix products, arithmetic and copies ran while one was open for 1% of the time, Pallas kernels for 8%

profile of v3, /device:TPU:2, one launch (start us, length us, event | category | flops | bytes accessed | tf_op | source)
XLA Modules:
  0.0 74.2 jit_solution(1861599789993234156)
XLA Ops:
  0.0 1.9 %collective-permute-start = (bf16[128,640]{1,0:T(8,128)(2,1)}, bf16[128,640]{1,0:T(8,128)(2,1)S(1)}, u32[]{:S(2)}, u32[]{:S(2)}) collective-permute-start(bf16[128,640]{1,0:T(8,128)(2,1)} %bitcast.11), channel_id=1, source_target_pairs={{0,1},{1,2},{2,3},{3,4},{4,5},{5,6},{6,7},{8,9},{9,10},{10,11},{11... | collective-permute-start | bytes 491528 | tf_op jit(solution)/shard_map/rows_to_heads/ppermute | solution.py:342
  1.9 0.8 %slice.4 = bf16[128,256]{1,0:T(8,128)(2,1)S(1)} slice(bf16[128,640]{1,0:T(8,128)(2,1)} %bitcast.12), slice={[0:128], [384:640]} | slice | bytes 131072 | tf_op jit(solution)/shard_map/rows_to_heads/slice | solution.py:343
  2.8 0.7 collective-permute-start.1
  3.4 0.0 copy-start
  3.4 2.5 %tokens_to_heads.1 = (bf16[1536,128]{1,0:T(8,128)(2,1)}, bf16[1408,128]{1,0:T(8,128)(2,1)}, bf16[1408,128]{1,0:T(8,128)(2,1)}, bf16[1408,128]{1,0:T(8,128)(2,1)}) custom-call(s32[1]{0:T(128)} %bitcast.seq_ref, bf16[512,1024]{1,0:T(8,128)(2,1)} %bitcast.18, bf16[128,1024]{1,0:T(8,128)(2,1)} %bitcast.19, bf16[128,640]{1,0:T(8,128)(2,1)} %bitcast.13), custom_call_target="tpu_custom_call" | custom-call | bytes 3145728 | tf_op jit(solution)/shard_map/tokens_to_heads/pallas_call | solution.py:36
  5.9 0.0 collective-permute-done.1.far_ref
  5.9 0.9 %collective-permute-done.near_ref = bf16[128,640]{1,0:T(8,128)(2,1)S(1)} collective-permute-done((bf16[128,640]{1,0:T(8,128)(2,1)}, bf16[128,640]{1,0:T(8,128)(2,1)S(1)}, u32[]{:S(2)}, u32[]{:S(2)}) %collective-permute-start) | collective-permute-done | bytes 163872 | tf_op jit(solution)/shard_map/rows_to_heads/ppermute | solution.py:342
  6.8 4.9 %collective-permute-start.2 = (bf16[1408,128]{1,0:T(8,128)(2,1)}, bf16[1408,128]{1,0:T(8,128)(2,1)S(1)}, u32[]{:S(2)}, u32[]{:S(2)}) collective-permute-start(bf16[1408,128]{1,0:T(8,128)(2,1)} %get-tuple-element.32), channel_id=1, source_target_pairs={{0,2},{1,3},{2,4},{3,5},{4,6},{5,7},{6,0},{7,1},{8,10},{9,11},{10,... | collective-permute-start | bytes 1081352 | tf_op jit(solution)/shard_map/tokens_to_heads/ppermute | solution.py:339
  11.8 5.3 %collective-permute-start.3 = (bf16[1408,128]{1,0:T(8,128)(2,1)}, bf16[1408,128]{1,0:T(8,128)(2,1)S(1)}, u32[]{:S(2)}, u32[]{:S(2)}) collective-permute-start(bf16[1408,128]{1,0:T(8,128)(2,1)} %get-tuple-element.33), channel_id=1, source_target_pairs={{0,4},{1,5},{2,6},{3,7},{4,0},{5,1},{6,2},{7,3},{8,12},{9,13},{10,... | collective-permute-start | bytes 1081352 | tf_op jit(solution)/shard_map/tokens_to_heads/ppermute | solution.py:339
  17.1 2.4 %collective-permute-start.4 = (bf16[1408,128]{1,0:T(8,128)(2,1)}, bf16[1408,128]{1,0:T(8,128)(2,1)S(1)}, u32[]{:S(2)}, u32[]{:S(2)}) collective-permute-start(bf16[1408,128]{1,0:T(8,128)(2,1)} %get-tuple-element.34), channel_id=1, source_target_pairs={{0,6},{1,7},{2,0},{3,1},{4,2},{5,3},{6,4},{7,5},{8,14},{9,15},{10,... | collective-permute-start | bytes 1081352 | tf_op jit(solution)/shard_map/tokens_to_heads/ppermute | solution.py:339
  19.6 1.2 %slots.1 = (bf16[1024,128]{1,0:T(8,128)(2,1)}, bf16[128,512]{1,0:T(8,128)(2,1)S(1)}) custom-call(s32[1]{0:T(128)} %bitcast.seq_ref, bf16[128,640]{1,0:T(8,128)(2,1)S(1)} %bitcast.14, bf16[128,640]{1,0:T(8,128)(2,1)S(1)} %collective-permute-done.near_ref, bf16[128,256]{1,0:T(8,128)(2,1)S(1)} %collective-permute-done.1.far_ref, s32[2,64]{1,0:T(2,128)S(1)} %bitcast.16), custom_call_target="tpu_custom_call" | custom-call | flops 33554432 | bytes 1048576 | tf_op jit(solution)/shard_map/slots/pallas_call | solution.py:36
  20.8 16.6 %all-to-all-start = ((bf16[64,16,128]{2,1,0:T(8,128)(2,1)}), bf16[64,16,128]{2,1,0:T(8,128)(2,1)S(1)}, u32[]{:S(2)}, u32[]{:S(2)}) async-start(bf16[64,16,128]{2,1,0:T(8,128)(2,1)} %bitcast.5), calls=%async_computation | async-start | bytes 524288 | tf_op jit(solution)/shard_map/rows_out/all_to_all | solution.py:373
  37.4 0.0 collective-permute-done.2.refs_1_
  37.4 0.0 collective-permute-done.3.refs_2_
  37.4 1.9 %collective-permute-start.5 = (bf16[1536,128]{1,0:T(8,128)(2,1)S(1)}, bf16[1536,128]{1,0:T(8,128)(2,1)S(1)}, u32[]{:S(2)}, u32[]{:S(2)}) collective-permute-start(bf16[1536,128]{1,0:T(8,128)(2,1)S(1)} %share_cores.1.mine_ref), channel_id=1, source_target_pairs={{0,1},{1,0},{2,3},{3,2},{4,5},{5,4},{6,7},{7,6},{8,9},{9,8},{10,11... | collective-permute-start | bytes 1179656 | tf_op jit(solution)/shard_map/share_cores/ppermute | solution.py:381
  39.4 11.5 %all-to-all-done = bf16[64,16,128]{2,1,0:T(8,128)(2,1)S(1)} async-done(((bf16[64,16,128]{2,1,0:T(8,128)(2,1)}), bf16[64,16,128]{2,1,0:T(8,128)(2,1)S(1)}, u32[]{:S(2)}, u32[]{:S(2)}) %all-to-all-start) | async-done | bytes 262176 | tf_op jit(solution)/shard_map/rows_out/all_to_all | solution.py:373
  50.9 2.7 %prefix_part.1 = bf16[1152,128]{1,0:T(8,128)(2,1)} custom-call(bf16[1024,128]{1,0:T(8,128)(2,1)S(1)} %bitcast.15, bf16[1536,128]{1,0:T(8,128)(2,1)S(1)} %share_cores.1.mine_ref, bf16[1536,128]{1,0:T(8,128)(2,1)S(1)} %collective-permute-done.5.other_ref), custom_call_target="tpu_custom_call" | custom-call | flops 536870912 | bytes 1048576 | tf_op jit(solution)/shard_map/prefix_part/pallas_call | solution.py:36
  53.6 4.8 %all-to-all-start.1 = ((bf16[64,9,2,128]{3,2,1,0:T(2,128)(2,1)}), bf16[64,9,2,128]{3,2,1,0:T(2,128)(2,1)S(1)}, u32[]{:S(2)}, u32[]{:S(2)}) async-start(bf16[64,9,2,128]{3,2,1,0:T(2,128)(2,1)} %bitcast.7), calls=%async_computation.1 | async-start | bytes 589824 | tf_op jit(solution)/shard_map/rows_back/all_to_all | solution.py:393
  58.4 2.0 %page_part.1 = (f32[136,640]{1,0:T(8,128)S(1)}, f32[136,640]{1,0:T(8,128)S(1)}) custom-call(s32[1]{0:T(128)} %bitcast.seq_ref, bf16[1536,128]{1,0:T(8,128)(2,1)S(1)} %share_cores.1.mine_ref, bf16[1536,128]{1,0:T(8,128)(2,1)S(1)} %collective-permute-done.5.other_ref, s32[2,64]{1,0:T(2,128)S(1)} %copy-done.3, bf16[1536,128]{1,0:T(8,128)(2,1)S(1)} %copy-done.1, ...), custom_call_target="tpu_custom_call" | custom-call | flops 1073741824 | bytes 2097152 | tf_op jit(solution)/shard_map/page_part/pallas_call | solution.py:36
  60.4 1.9 %collective-permute-start.6 = (f32[136,640]{1,0:T(8,128)S(1)}, f32[136,640]{1,0:T(8,128)S(1)}, u32[]{:S(2)}, u32[]{:S(2)}) collective-permute-start(f32[136,640]{1,0:T(8,128)S(1)} %get-tuple-element.36), channel_id=1, source_target_pairs={{0,1},{1,0},{2,3},{3,2},{4,5},{5,4},{6,7},{7,6},{8,9},{9,8},{10,11... | collective-permute-start | bytes 1044488 | tf_op jit(solution)/shard_map/page_part/ppermute | solution.py:403
  62.3 1.6 %collective-permute-done.6.got_ref = f32[136,640]{1,0:T(8,128)S(1)} collective-permute-done((f32[136,640]{1,0:T(8,128)S(1)}, f32[136,640]{1,0:T(8,128)S(1)}, u32[]{:S(2)}, u32[]{:S(2)}) %collective-permute-start.6) | collective-permute-done | bytes 348192 | tf_op jit(solution)/shard_map/page_part/ppermute | solution.py:403
  63.9 0.5 page_merge.1
  64.4 8.2 %all-to-all-done.1 = bf16[64,9,2,128]{3,2,1,0:T(2,128)(2,1)S(1)} async-done(((bf16[64,9,2,128]{3,2,1,0:T(2,128)(2,1)}), bf16[64,9,2,128]{3,2,1,0:T(2,128)(2,1)S(1)}, u32[]{:S(2)}, u32[]{:S(2)}) %all-to-all-start.1) | async-done | bytes 294944 | tf_op jit(solution)/shard_map/rows_back/all_to_all | solution.py:393
  72.6 1.6 %finish.1 = bf16[128,512]{1,0:T(8,128)(2,1)} custom-call(bf16[1152,128]{1,0:T(8,128)(2,1)S(1)} %bitcast.10, f32[128,512]{1,0:T(8,128)S(1)} %get-tuple-element.37.part_ref, f32[128,128]{1,0:T(8,128)S(1)} %get-tuple-element.38.stat_ref, bf16[128,320]{1,0:T(8,128)(2,1)S(1)} %get-tuple-element.39.pick_ref, f32[128,512]{1,0:T(8,128)S(1)} %get-tuple-element.40.mask_ref), custom_call_target="tpu_custom_call" | custom-call | flops 33554432 | bytes 1048576 | tf_op jit(solution)/shard_map/finish/pallas_call | solution.py:36
  (10 shorter events, 0.1 us)
Async XLA Ops:
  0.0 6.8 %collective-permute-start = (bf16[128,640]{1,0:T(8,128)(2,1)}, bf16[128,640]{1,0:T(8,128)(2,1)S(1)}, u32[]{:S(2)}, u32[]{:S(2)}) collective-permute-start(bf16[128,640]{1,0:T(8,128)(2,1)} %bitcast.11), channel_id=1, source_target_pairs={{0,1},{1,2},{2,3},{3,4},{4,5},{5,6},{6,7},{8,9},{9,10},{10,11},{11... | collective-permute-start | bytes 491528 | tf_op jit(solution)/shard_map/rows_to_heads/ppermute | solution.py:342
  2.8 3.1 %collective-permute-start.1 = (bf16[128,256]{1,0:T(8,128)(2,1)S(1)}, bf16[128,256]{1,0:T(8,128)(2,1)S(1)}, u32[]{:S(2)}, u32[]{:S(2)}) collective-permute-start(bf16[128,256]{1,0:T(8,128)(2,1)S(1)} %slice.4), channel_id=1, source_target_pairs={{4,6},{5,7},{12,14},{13,15},{20,22},{21,23},{28,30},{29,31},{36,38... | collective-permute-start | bytes 196616 | tf_op jit(solution)/shard_map/rows_to_heads/ppermute | solution.py:343
  3.4 16.1 %copy-start = (bf16[2,64,640]{2,1,0:T(8,128)(2,1)S(1)}, bf16[2,64,640]{2,1,0:T(8,128)(2,1)}, u32[]{:S(2)}) copy-start(bf16[2,64,640]{2,1,0:T(8,128)(2,1)} %param.5) | copy-start | bytes 491524
  6.8 12.7 %copy-start.2 = (s32[2,64,1]{1,2,0:T(1,128)S(1)}, s32[2,64,1]{1,2,0:T(1,128)}, u32[]{:S(2)}) copy-start(s32[2,64,1]{1,2,0:T(1,128)} %param.6) | copy-start | bytes 1540
  6.8 30.5 %collective-permute-start.2 = (bf16[1408,128]{1,0:T(8,128)(2,1)}, bf16[1408,128]{1,0:T(8,128)(2,1)S(1)}, u32[]{:S(2)}, u32[]{:S(2)}) collective-permute-start(bf16[1408,128]{1,0:T(8,128)(2,1)} %get-tuple-element.32), channel_id=1, source_target_pairs={{0,2},{1,3},{2,4},{3,5},{4,6},{5,7},{6,0},{7,1},{8,10},{9,11},{10,... | collective-permute-start | bytes 1081352 | tf_op jit(solution)/shard_map/tokens_to_heads/ppermute | solution.py:339
  11.8 25.6 %collective-permute-start.3 = (bf16[1408,128]{1,0:T(8,128)(2,1)}, bf16[1408,128]{1,0:T(8,128)(2,1)S(1)}, u32[]{:S(2)}, u32[]{:S(2)}) collective-permute-start(bf16[1408,128]{1,0:T(8,128)(2,1)} %get-tuple-element.33), channel_id=1, source_target_pairs={{0,4},{1,5},{2,6},{3,7},{4,0},{5,1},{6,2},{7,3},{8,12},{9,13},{10,... | collective-permute-start | bytes 1081352 | tf_op jit(solution)/shard_map/tokens_to_heads/ppermute | solution.py:339
  17.1 20.3 %collective-permute-start.4 = (bf16[1408,128]{1,0:T(8,128)(2,1)}, bf16[1408,128]{1,0:T(8,128)(2,1)S(1)}, u32[]{:S(2)}, u32[]{:S(2)}) collective-permute-start(bf16[1408,128]{1,0:T(8,128)(2,1)} %get-tuple-element.34), channel_id=1, source_target_pairs={{0,6},{1,7},{2,0},{3,1},{4,2},{5,3},{6,4},{7,5},{8,14},{9,15},{10,... | collective-permute-start | bytes 1081352 | tf_op jit(solution)/shard_map/tokens_to_heads/ppermute | solution.py:339
  19.6 17.8 %copy-start.1 = (bf16[1536,128]{1,0:T(8,128)(2,1)S(1)}, bf16[1536,128]{1,0:T(8,128)(2,1)}, u32[]{:S(2)}) copy-start(bf16[1536,128]{1,0:T(8,128)(2,1)} %get-tuple-element.31.refs_0_) | copy-start | bytes 1179652
  20.8 30.1 %all-to-all-start = ((bf16[64,16,128]{2,1,0:T(8,128)(2,1)}), bf16[64,16,128]{2,1,0:T(8,128)(2,1)S(1)}, u32[]{:S(2)}, u32[]{:S(2)}) async-start(bf16[64,16,128]{2,1,0:T(8,128)(2,1)} %bitcast.5), calls=%async_computation | async-start | bytes 524288 | tf_op jit(solution)/shard_map/rows_out/all_to_all | solution.py:373
  37.4 13.5 %collective-permute-start.5 = (bf16[1536,128]{1,0:T(8,128)(2,1)S(1)}, bf16[1536,128]{1,0:T(8,128)(2,1)S(1)}, u32[]{:S(2)}, u32[]{:S(2)}) collective-permute-start(bf16[1536,128]{1,0:T(8,128)(2,1)S(1)} %share_cores.1.mine_ref), channel_id=1, source_target_pairs={{0,1},{1,0},{2,3},{3,2},{4,5},{5,4},{6,7},{7,6},{8,9},{9,8},{10,11... | collective-permute-start | bytes 1179656 | tf_op jit(solution)/shard_map/share_cores/ppermute | solution.py:381
  53.6 4.8 %copy-start.3 = (s32[2,64]{1,0:T(2,128)S(1)}, s32[2,64]{1,0:T(2,128)}, u32[]{:S(2)}) copy-start(s32[2,64]{1,0:T(2,128)} %parent_ref.1) | copy-start | bytes 1540
  53.6 18.9 %all-to-all-start.1 = ((bf16[64,9,2,128]{3,2,1,0:T(2,128)(2,1)}), bf16[64,9,2,128]{3,2,1,0:T(2,128)(2,1)S(1)}, u32[]{:S(2)}, u32[]{:S(2)}) async-start(bf16[64,9,2,128]{3,2,1,0:T(2,128)(2,1)} %bitcast.7), calls=%async_computation.1 | async-start | bytes 589824 | tf_op jit(solution)/shard_map/rows_back/all_to_all | solution.py:393
  60.4 3.6 %collective-permute-start.6 = (f32[136,640]{1,0:T(8,128)S(1)}, f32[136,640]{1,0:T(8,128)S(1)}, u32[]{:S(2)}, u32[]{:S(2)}) collective-permute-start(f32[136,640]{1,0:T(8,128)S(1)} %get-tuple-element.36), channel_id=1, source_target_pairs={{0,1},{1,0},{2,3},{3,2},{4,5},{5,4},{6,7},{7,6},{8,9},{9,8},{10,11... | collective-permute-start | bytes 1044488 | tf_op jit(solution)/shard_map/page_part/ppermute | solution.py:403

commit v4 on v3

--- a/solution.py
+++ b/solution.py
@@ -357,7 +357,9 @@
             vmem=58,
             out="r",
         )
-        *split, near, far = lax.optimization_barrier((*split, near, far))
+        split = list(split)
+        split[1], near = lax.optimization_barrier((split[1], near))
+        split[2], split[3], far = lax.optimization_barrier((split[2], split[3], far))
         pieces = [split[0]] + [turn(split[k], k) for k in range(1, 4)]
     with jax.named_scope("slots"):
         sent, query = call(

time: 74.6 us -> 73.9 us (level)
  waiting for transfers between devices: 22.2 us -> 21.3 us
    ppermute x1, waiting for transfers between devices: 0.92 us -> 0.01 us  [body(): near = lax.ppermute(own, 'seq', [(i, i + 1) for i in range(seq_count - 1)])]
  transfers between devices with their start and end apart: 9 -> 9, of which waited for: 4 -> 3; matrix products, arithmetic and copies ran while one was open for 1% -> 1% of each run, Pallas kernels for 8% -> 8%
where the time goes in v4:
time: 73.9 us; the launch traced here: 73.4 us
  starting transfers between devices  40.6 us (55%)
  waiting for transfers between devices  21.3 us (29%)
  Pallas kernels  10.4 us (14%)
  local copies, waits for them, and re-layouts  0.87 us (1%)
    all_to_all x1, starting transfers between devices, body(): lax.all_to_all(sent, 'prompt', 0, 0, tiled=True).reshape(slots, DH)  16.6 us
    ppermute x3, starting transfers between devices, turn(): lax.ppermute(value, 'seq', [(i, (i + 2 * k) % seq_count) for i in range(s...  12.9 us
    all_to_all x1, waiting for transfers between devices, body(): lax.all_to_all(sent, 'prompt', 0, 0, tiled=True).reshape(slots, DH)  11.5 us
    pallas_call x7, Pallas kernels, call(): pl.pallas_call(kernel, out_shape=(outs,) if single else outs, in_specs=[s...  10.4 us
    all_to_all x1, waiting for transfers between devices, body(): back = lax.all_to_all(part, 'prompt', 0, 0, tiled=True).reshape(-1, DH)  8.17 us
    all_to_all x1, starting transfers between devices, body(): back = lax.all_to_all(part, 'prompt', 0, 0, tiled=True).reshape(-1, DH)  4.75 us
    ppermute x1, starting transfers between devices, body(): other = lax.ppermute(shared, 'seq', swap)  1.92 us
    ppermute x1, starting transfers between devices, body(): got = lax.ppermute(lent, 'seq', swap)  1.92 us
  transfers between devices with their start and end apart: 9, of which 3 were waited for; matrix products, arithmetic and copies ran while one was open for 1% of the time, Pallas kernels for 8%

profile of v4, /device:TPU:2, one launch (start us, length us, event | category | flops | bytes accessed | tf_op | source)
XLA Modules:
  0.0 73.4 jit_solution(3467448257161306095)
XLA Ops:
  0.0 1.9 %collective-permute-start = (bf16[128,640]{1,0:T(8,128)(2,1)}, bf16[128,640]{1,0:T(8,128)(2,1)S(1)}, u32[]{:S(2)}, u32[]{:S(2)}) collective-permute-start(bf16[128,640]{1,0:T(8,128)(2,1)} %bitcast.11), channel_id=1, source_target_pairs={{0,1},{1,2},{2,3},{3,4},{4,5},{5,6},{6,7},{8,9},{9,10},{10,11},{11... | collective-permute-start | bytes 491528 | tf_op jit(solution)/shard_map/rows_to_heads/ppermute | solution.py:342
  1.9 0.8 %slice.4 = bf16[128,256]{1,0:T(8,128)(2,1)S(1)} slice(bf16[128,640]{1,0:T(8,128)(2,1)} %bitcast.12), slice={[0:128], [384:640]} | slice | bytes 131072 | tf_op jit(solution)/shard_map/rows_to_heads/slice | solution.py:343
  2.8 0.7 collective-permute-start.1
  3.4 0.0 copy-start
  3.4 2.5 %tokens_to_heads.1 = (bf16[1536,128]{1,0:T(8,128)(2,1)}, bf16[1408,128]{1,0:T(8,128)(2,1)}, bf16[1408,128]{1,0:T(8,128)(2,1)}, bf16[1408,128]{1,0:T(8,128)(2,1)}) custom-call(s32[1]{0:T(128)} %bitcast.seq_ref, bf16[512,1024]{1,0:T(8,128)(2,1)} %bitcast.18, bf16[128,1024]{1,0:T(8,128)(2,1)} %bitcast.19, bf16[128,640]{1,0:T(8,128)(2,1)} %bitcast.13), custom_call_target="tpu_custom_call" | custom-call | bytes 3145728 | tf_op jit(solution)/shard_map/tokens_to_heads/pallas_call | solution.py:36
  5.9 7.0 %collective-permute-start.3 = (bf16[1408,128]{1,0:T(8,128)(2,1)}, bf16[1408,128]{1,0:T(8,128)(2,1)S(1)}, u32[]{:S(2)}, u32[]{:S(2)}) collective-permute-start(bf16[1408,128]{1,0:T(8,128)(2,1)} %get-tuple-element.31), channel_id=1, source_target_pairs={{0,4},{1,5},{2,6},{3,7},{4,0},{5,1},{6,2},{7,3},{8,12},{9,13},{10,... | collective-permute-start | bytes 1081352 | tf_op jit(solution)/shard_map/tokens_to_heads/ppermute | solution.py:339
  12.9 2.8 %collective-permute-start.4 = (bf16[1408,128]{1,0:T(8,128)(2,1)}, bf16[1408,128]{1,0:T(8,128)(2,1)S(1)}, u32[]{:S(2)}, u32[]{:S(2)}) collective-permute-start(bf16[1408,128]{1,0:T(8,128)(2,1)} %get-tuple-element.32), channel_id=1, source_target_pairs={{0,6},{1,7},{2,0},{3,1},{4,2},{5,3},{6,4},{7,5},{8,14},{9,15},{10,... | collective-permute-start | bytes 1081352 | tf_op jit(solution)/shard_map/tokens_to_heads/ppermute | solution.py:339
  15.8 0.0 copy-start.2
  15.8 3.0 %collective-permute-start.2 = (bf16[1408,128]{1,0:T(8,128)(2,1)}, bf16[1408,128]{1,0:T(8,128)(2,1)S(1)}, u32[]{:S(2)}, u32[]{:S(2)}) collective-permute-start(bf16[1408,128]{1,0:T(8,128)(2,1)} %get-tuple-element.30), channel_id=1, source_target_pairs={{0,2},{1,3},{2,4},{3,5},{4,6},{5,7},{6,0},{7,1},{8,10},{9,11},{10,... | collective-permute-start | bytes 1081352 | tf_op jit(solution)/shard_map/tokens_to_heads/ppermute | solution.py:339
  18.9 1.2 %slots.1 = (bf16[1024,128]{1,0:T(8,128)(2,1)}, bf16[128,512]{1,0:T(8,128)(2,1)S(1)}) custom-call(s32[1]{0:T(128)} %bitcast.seq_ref, bf16[128,640]{1,0:T(8,128)(2,1)S(1)} %bitcast.14, bf16[128,640]{1,0:T(8,128)(2,1)S(1)} %collective-permute-done.near_ref, bf16[128,256]{1,0:T(8,128)(2,1)S(1)} %collective-permute-done.1.far_ref, s32[2,64]{1,0:T(2,128)S(1)} %bitcast.16), custom_call_target="tpu_custom_call" | custom-call | flops 33554432 | bytes 1048576 | tf_op jit(solution)/shard_map/slots/pallas_call | solution.py:36
  20.0 16.6 %all-to-all-start = ((bf16[64,16,128]{2,1,0:T(8,128)(2,1)}), bf16[64,16,128]{2,1,0:T(8,128)(2,1)S(1)}, u32[]{:S(2)}, u32[]{:S(2)}) async-start(bf16[64,16,128]{2,1,0:T(8,128)(2,1)} %bitcast.5), calls=%async_computation | async-start | bytes 524288 | tf_op jit(solution)/shard_map/rows_out/all_to_all | solution.py:375
  36.6 0.0 collective-permute-done.3.refs_2_
  36.7 0.0 collective-permute-done.2.refs_1_
  36.7 1.9 %collective-permute-start.5 = (bf16[1536,128]{1,0:T(8,128)(2,1)S(1)}, bf16[1536,128]{1,0:T(8,128)(2,1)S(1)}, u32[]{:S(2)}, u32[]{:S(2)}) collective-permute-start(bf16[1536,128]{1,0:T(8,128)(2,1)S(1)} %share_cores.1.mine_ref), channel_id=1, source_target_pairs={{0,1},{1,0},{2,3},{3,2},{4,5},{5,4},{6,7},{7,6},{8,9},{9,8},{10,11... | collective-permute-start | bytes 1179656 | tf_op jit(solution)/shard_map/share_cores/ppermute | solution.py:383
  38.7 11.5 %all-to-all-done = bf16[64,16,128]{2,1,0:T(8,128)(2,1)S(1)} async-done(((bf16[64,16,128]{2,1,0:T(8,128)(2,1)}), bf16[64,16,128]{2,1,0:T(8,128)(2,1)S(1)}, u32[]{:S(2)}, u32[]{:S(2)}) %all-to-all-start) | async-done | bytes 262176 | tf_op jit(solution)/shard_map/rows_out/all_to_all | solution.py:375
  50.2 0.0 collective-permute-done.5.other_ref
  50.2 2.7 %prefix_part.1 = bf16[1152,128]{1,0:T(8,128)(2,1)} custom-call(bf16[1024,128]{1,0:T(8,128)(2,1)S(1)} %bitcast.15, bf16[1536,128]{1,0:T(8,128)(2,1)S(1)} %share_cores.1.mine_ref, bf16[1536,128]{1,0:T(8,128)(2,1)S(1)} %collective-permute-done.5.other_ref), custom_call_target="tpu_custom_call" | custom-call | flops 536870912 | bytes 1048576 | tf_op jit(solution)/shard_map/prefix_part/pallas_call | solution.py:36
  52.9 4.8 %all-to-all-start.1 = ((bf16[64,9,2,128]{3,2,1,0:T(2,128)(2,1)}), bf16[64,9,2,128]{3,2,1,0:T(2,128)(2,1)S(1)}, u32[]{:S(2)}, u32[]{:S(2)}) async-start(bf16[64,9,2,128]{3,2,1,0:T(2,128)(2,1)} %bitcast.7), calls=%async_computation.1 | async-start | bytes 589824 | tf_op jit(solution)/shard_map/rows_back/all_to_all | solution.py:395
  57.7 2.0 %page_part.1 = (f32[136,640]{1,0:T(8,128)S(1)}, f32[136,640]{1,0:T(8,128)S(1)}) custom-call(s32[1]{0:T(128)} %bitcast.seq_ref, bf16[1536,128]{1,0:T(8,128)(2,1)S(1)} %share_cores.1.mine_ref, bf16[1536,128]{1,0:T(8,128)(2,1)S(1)} %collective-permute-done.5.other_ref, s32[2,64]{1,0:T(2,128)S(1)} %copy-done.3, bf16[1536,128]{1,0:T(8,128)(2,1)S(1)} %copy-done.1, ...), custom_call_target="tpu_custom_call" | custom-call | flops 1073741824 | bytes 2097152 | tf_op jit(solution)/shard_map/page_part/pallas_call | solution.py:36
  59.7 1.9 %collective-permute-start.6 = (f32[136,640]{1,0:T(8,128)S(1)}, f32[136,640]{1,0:T(8,128)S(1)}, u32[]{:S(2)}, u32[]{:S(2)}) collective-permute-start(f32[136,640]{1,0:T(8,128)S(1)} %get-tuple-element.34), channel_id=1, source_target_pairs={{0,1},{1,0},{2,3},{3,2},{4,5},{5,4},{6,7},{7,6},{8,9},{9,8},{10,11... | collective-permute-start | bytes 1044488 | tf_op jit(solution)/shard_map/page_part/ppermute | solution.py:405
  61.6 1.6 %collective-permute-done.6.got_ref = f32[136,640]{1,0:T(8,128)S(1)} collective-permute-done((f32[136,640]{1,0:T(8,128)S(1)}, f32[136,640]{1,0:T(8,128)S(1)}, u32[]{:S(2)}, u32[]{:S(2)}) %collective-permute-start.6) | collective-permute-done | bytes 348192 | tf_op jit(solution)/shard_map/page_part/ppermute | solution.py:405
  63.2 0.5 page_merge.1
  63.7 8.2 %all-to-all-done.1 = bf16[64,9,2,128]{3,2,1,0:T(2,128)(2,1)S(1)} async-done(((bf16[64,9,2,128]{3,2,1,0:T(2,128)(2,1)}), bf16[64,9,2,128]{3,2,1,0:T(2,128)(2,1)S(1)}, u32[]{:S(2)}, u32[]{:S(2)}) %all-to-all-start.1) | async-done | bytes 294944 | tf_op jit(solution)/shard_map/rows_back/all_to_all | solution.py:395
  71.9 1.6 %finish.1 = bf16[128,512]{1,0:T(8,128)(2,1)} custom-call(bf16[1152,128]{1,0:T(8,128)(2,1)S(1)} %bitcast.10, f32[128,512]{1,0:T(8,128)S(1)} %get-tuple-element.35.part_ref, f32[128,128]{1,0:T(8,128)S(1)} %get-tuple-element.36.stat_ref, bf16[128,320]{1,0:T(8,128)(2,1)S(1)} %get-tuple-element.37.pick_ref, f32[128,512]{1,0:T(8,128)S(1)} %get-tuple-element.38.mask_ref), custom_call_target="tpu_custom_call" | custom-call | flops 33554432 | bytes 1048576 | tf_op jit(solution)/shard_map/finish/pallas_call | solution.py:36
  (10 shorter events, 0.1 us)
Async XLA Ops:
  0.0 15.7 %collective-permute-start = (bf16[128,640]{1,0:T(8,128)(2,1)}, bf16[128,640]{1,0:T(8,128)(2,1)S(1)}, u32[]{:S(2)}, u32[]{:S(2)}) collective-permute-start(bf16[128,640]{1,0:T(8,128)(2,1)} %bitcast.11), channel_id=1, source_target_pairs={{0,1},{1,2},{2,3},{3,4},{4,5},{5,6},{6,7},{8,9},{9,10},{10,11},{11... | collective-permute-start | bytes 491528 | tf_op jit(solution)/shard_map/rows_to_heads/ppermute | solution.py:342
  2.8 3.1 %collective-permute-start.1 = (bf16[128,256]{1,0:T(8,128)(2,1)S(1)}, bf16[128,256]{1,0:T(8,128)(2,1)S(1)}, u32[]{:S(2)}, u32[]{:S(2)}) collective-permute-start(bf16[128,256]{1,0:T(8,128)(2,1)S(1)} %slice.4), channel_id=1, source_target_pairs={{4,6},{5,7},{12,14},{13,15},{20,22},{21,23},{28,30},{29,31},{36,38... | collective-permute-start | bytes 196616 | tf_op jit(solution)/shard_map/rows_to_heads/ppermute | solution.py:343
  3.4 15.4 %copy-start = (bf16[2,64,640]{2,1,0:T(8,128)(2,1)S(1)}, bf16[2,64,640]{2,1,0:T(8,128)(2,1)}, u32[]{:S(2)}) copy-start(bf16[2,64,640]{2,1,0:T(8,128)(2,1)} %param.5) | copy-start | bytes 491524
  5.9 30.7 %collective-permute-start.3 = (bf16[1408,128]{1,0:T(8,128)(2,1)}, bf16[1408,128]{1,0:T(8,128)(2,1)S(1)}, u32[]{:S(2)}, u32[]{:S(2)}) collective-permute-start(bf16[1408,128]{1,0:T(8,128)(2,1)} %get-tuple-element.31), channel_id=1, source_target_pairs={{0,4},{1,5},{2,6},{3,7},{4,0},{5,1},{6,2},{7,3},{8,12},{9,13},{10,... | collective-permute-start | bytes 1081352 | tf_op jit(solution)/shard_map/tokens_to_heads/ppermute | solution.py:339
  12.9 23.7 %collective-permute-start.4 = (bf16[1408,128]{1,0:T(8,128)(2,1)}, bf16[1408,128]{1,0:T(8,128)(2,1)S(1)}, u32[]{:S(2)}, u32[]{:S(2)}) collective-permute-start(bf16[1408,128]{1,0:T(8,128)(2,1)} %get-tuple-element.32), channel_id=1, source_target_pairs={{0,6},{1,7},{2,0},{3,1},{4,2},{5,3},{6,4},{7,5},{8,14},{9,15},{10,... | collective-permute-start | bytes 1081352 | tf_op jit(solution)/shard_map/tokens_to_heads/ppermute | solution.py:339
  15.8 3.1 %copy-start.2 = (s32[2,64,1]{1,2,0:T(1,128)S(1)}, s32[2,64,1]{1,2,0:T(1,128)}, u32[]{:S(2)}) copy-start(s32[2,64,1]{1,2,0:T(1,128)} %param.6) | copy-start | bytes 1540
  15.8 20.9 %collective-permute-start.2 = (bf16[1408,128]{1,0:T(8,128)(2,1)}, bf16[1408,128]{1,0:T(8,128)(2,1)S(1)}, u32[]{:S(2)}, u32[]{:S(2)}) collective-permute-start(bf16[1408,128]{1,0:T(8,128)(2,1)} %get-tuple-element.30), channel_id=1, source_target_pairs={{0,2},{1,3},{2,4},{3,5},{4,6},{5,7},{6,0},{7,1},{8,10},{9,11},{10,... | collective-permute-start | bytes 1081352 | tf_op jit(solution)/shard_map/tokens_to_heads/ppermute | solution.py:339
  18.8 17.8 %copy-start.1 = (bf16[1536,128]{1,0:T(8,128)(2,1)S(1)}, bf16[1536,128]{1,0:T(8,128)(2,1)}, u32[]{:S(2)}) copy-start(bf16[1536,128]{1,0:T(8,128)(2,1)} %get-tuple-element.29.refs_0_) | copy-start | bytes 1179652
  20.0 30.1 %all-to-all-start = ((bf16[64,16,128]{2,1,0:T(8,128)(2,1)}), bf16[64,16,128]{2,1,0:T(8,128)(2,1)S(1)}, u32[]{:S(2)}, u32[]{:S(2)}) async-start(bf16[64,16,128]{2,1,0:T(8,128)(2,1)} %bitcast.5), calls=%async_computation | async-start | bytes 524288 | tf_op jit(solution)/shard_map/rows_out/all_to_all | solution.py:375
  36.7 13.4 %collective-permute-start.5 = (bf16[1536,128]{1,0:T(8,128)(2,1)S(1)}, bf16[1536,128]{1,0:T(8,128)(2,1)S(1)}, u32[]{:S(2)}, u32[]{:S(2)}) collective-permute-start(bf16[1536,128]{1,0:T(8,128)(2,1)S(1)} %share_cores.1.mine_ref), channel_id=1, source_target_pairs={{0,1},{1,0},{2,3},{3,2},{4,5},{5,4},{6,7},{7,6},{8,9},{9,8},{10,11... | collective-permute-start | bytes 1179656 | tf_op jit(solution)/shard_map/share_cores/ppermute | solution.py:383
  52.9 4.8 %copy-start.3 = (s32[2,64]{1,0:T(2,128)S(1)}, s32[2,64]{1,0:T(2,128)}, u32[]{:S(2)}) copy-start(s32[2,64]{1,0:T(2,128)} %parent_ref.1) | copy-start | bytes 1540
  52.9 19.0 %all-to-all-start.1 = ((bf16[64,9,2,128]{3,2,1,0:T(2,128)(2,1)}), bf16[64,9,2,128]{3,2,1,0:T(2,128)(2,1)S(1)}, u32[]{:S(2)}, u32[]{:S(2)}) async-start(bf16[64,9,2,128]{3,2,1,0:T(2,128)(2,1)} %bitcast.7), calls=%async_computation.1 | async-start | bytes 589824 | tf_op jit(solution)/shard_map/rows_back/all_to_all | solution.py:395
  59.7 3.6 %collective-permute-start.6 = (f32[136,640]{1,0:T(8,128)S(1)}, f32[136,640]{1,0:T(8,128)S(1)}, u32[]{:S(2)}, u32[]{:S(2)}) collective-permute-start(f32[136,640]{1,0:T(8,128)S(1)} %get-tuple-element.34), channel_id=1, source_target_pairs={{0,1},{1,0},{2,3},{3,2},{4,5},{5,4},{6,7},{7,6},{8,9},{9,8},{10,11... | collective-permute-start | bytes 1044488 | tf_op jit(solution)/shard_map/page_part/ppermute | solution.py:405

commit v5 on v4

--- a/solution.py
+++ b/solution.py
@@ -122,7 +122,7 @@
     width = own_ref.shape[1]
     heads = query_ref.shape[1] // DH
     count = sent_ref.shape[0] // heads
-    line[:, 3 * DH : width] = far_ref[...]
+    line[:, 3 * DH : width] = far_ref[:, 3 * DH :]
     line[:, width : 2 * width] = near_ref[...]
     line[:, 2 * width :] = own_ref[...]
     first = pl.multiple_of((10 - seq_ref[0]) * DH, DH)
@@ -340,7 +340,7 @@
 
     with jax.named_scope("rows_to_heads"):
         near = lax.ppermute(own, "seq", [(i, i + 1) for i in range(seq_count - 1)])
-        far = lax.ppermute(own[:, 3 * DH :], "seq", [(4, 6), (5, 7)])
+        far = lax.ppermute(own, "seq", [(4, 6), (5, 7)])
     with jax.named_scope("tokens_to_heads"):
         count = pages.shape[0] * pages.shape[1]
         pre = prefix_kv.shape[1]

time: 73.9 us -> 75.5 us (1.022)
  waiting for transfers between devices: 21.3 us -> 23.2 us
  local copies, waits for them, and re-layouts: 0.87 us -> 0.02 us
    ppermute x1, waiting for transfers between devices: 0.01 us -> 1.77 us  [body(): near = lax.ppermute(own, 'seq', [(i, i + 1) for i in range(seq_count - 1)])]
    slice x1 -> x0, local copies, waits for them, and re-layouts: 0.85 us -> none  [body(): far = lax.ppermute(own[:, 3 * DH:], 'seq', [(4, 6), (5, 7)])]
  transfers between devices with their start and end apart: 9 -> 9, of which waited for: 3 -> 4; matrix products, arithmetic and copies ran while one was open for 1% -> 0% of each run, Pallas kernels for 8% -> 8%
where the time goes in v5:
time: 75.5 us; the launch traced here: 75 us
  starting transfers between devices  41.3 us (55%)
  waiting for transfers between devices  23.2 us (31%)
  Pallas kernels  10.4 us (14%)
    all_to_all x1, starting transfers between devices, body(): lax.all_to_all(sent, 'prompt', 0, 0, tiled=True).reshape(slots, DH)  16.6 us
    ppermute x3, starting transfers between devices, turn(): lax.ppermute(value, 'seq', [(i, (i + 2 * k) % seq_count) for i in range(s...  13.5 us
    all_to_all x1, waiting for transfers between devices, body(): lax.all_to_all(sent, 'prompt', 0, 0, tiled=True).reshape(slots, DH)  11.8 us
    pallas_call x7, Pallas kernels, call(): pl.pallas_call(kernel, out_shape=(outs,) if single else outs, in_specs=[s...  10.4 us
    all_to_all x1, waiting for transfers between devices, body(): back = lax.all_to_all(part, 'prompt', 0, 0, tiled=True).reshape(-1, DH)  7.98 us
    all_to_all x1, starting transfers between devices, body(): back = lax.all_to_all(part, 'prompt', 0, 0, tiled=True).reshape(-1, DH)  4.75 us
    ppermute x1, starting transfers between devices, body(): got = lax.ppermute(lent, 'seq', swap)  1.92 us
    ppermute x1, starting transfers between devices, body(): other = lax.ppermute(shared, 'seq', swap)  1.92 us
  transfers between devices with their start and end apart: 9, of which 4 were waited for; matrix products, arithmetic and copies ran while one was open for 0% of the time, Pallas kernels for 8%

profile of v5, /device:TPU:2, one launch (start us, length us, event | category | flops | bytes accessed | tf_op | source)
XLA Modules:
  0.0 75.0 jit_solution(13723141579020015923)
XLA Ops:
  0.0 1.9 %collective-permute-start = (bf16[128,640]{1,0:T(8,128)(2,1)}, bf16[128,640]{1,0:T(8,128)(2,1)S(1)}, u32[]{:S(2)}, u32[]{:S(2)}) collective-permute-start(bf16[128,640]{1,0:T(8,128)(2,1)} %bitcast.11), channel_id=1, source_target_pairs={{0,1},{1,2},{2,3},{3,4},{4,5},{5,6},{6,7},{8,9},{9,10},{10,11},{11... | collective-permute-start | bytes 491528 | tf_op jit(solution)/shard_map/rows_to_heads/ppermute | solution.py:342
  1.9 0.7 collective-permute-start.1
  2.6 2.4 %tokens_to_heads.1 = (bf16[1536,128]{1,0:T(8,128)(2,1)}, bf16[1408,128]{1,0:T(8,128)(2,1)}, bf16[1408,128]{1,0:T(8,128)(2,1)}, bf16[1408,128]{1,0:T(8,128)(2,1)}) custom-call(s32[1]{0:T(128)} %bitcast.seq_ref, bf16[512,1024]{1,0:T(8,128)(2,1)} %bitcast.18, bf16[128,1024]{1,0:T(8,128)(2,1)} %bitcast.19, bf16[128,640]{1,0:T(8,128)(2,1)} %bitcast.13), custom_call_target="tpu_custom_call" | custom-call | bytes 3145728 | tf_op jit(solution)/shard_map/tokens_to_heads/pallas_call | solution.py:36
  5.1 1.8 %collective-permute-done.near_ref = bf16[128,640]{1,0:T(8,128)(2,1)S(1)} collective-permute-done((bf16[128,640]{1,0:T(8,128)(2,1)}, bf16[128,640]{1,0:T(8,128)(2,1)S(1)}, u32[]{:S(2)}, u32[]{:S(2)}) %collective-permute-start) | collective-permute-done | bytes 163872 | tf_op jit(solution)/shard_map/rows_to_heads/ppermute | solution.py:342
  6.8 0.0 collective-permute-done.1.far_ref
  6.8 7.7 %collective-permute-start.3 = (bf16[1408,128]{1,0:T(8,128)(2,1)}, bf16[1408,128]{1,0:T(8,128)(2,1)S(1)}, u32[]{:S(2)}, u32[]{:S(2)}) collective-permute-start(bf16[1408,128]{1,0:T(8,128)(2,1)} %get-tuple-element.31), channel_id=1, source_target_pairs={{0,4},{1,5},{2,6},{3,7},{4,0},{5,1},{6,2},{7,3},{8,12},{9,13},{10,... | collective-permute-start | bytes 1081352 | tf_op jit(solution)/shard_map/tokens_to_heads/ppermute | solution.py:339
  14.5 2.2 %collective-permute-start.4 = (bf16[1408,128]{1,0:T(8,128)(2,1)}, bf16[1408,128]{1,0:T(8,128)(2,1)S(1)}, u32[]{:S(2)}, u32[]{:S(2)}) collective-permute-start(bf16[1408,128]{1,0:T(8,128)(2,1)} %get-tuple-element.32), channel_id=1, source_target_pairs={{0,6},{1,7},{2,0},{3,1},{4,2},{5,3},{6,4},{7,5},{8,14},{9,15},{10,... | collective-permute-start | bytes 1081352 | tf_op jit(solution)/shard_map/tokens_to_heads/ppermute | solution.py:339
  16.7 3.7 %collective-permute-start.2 = (bf16[1408,128]{1,0:T(8,128)(2,1)}, bf16[1408,128]{1,0:T(8,128)(2,1)S(1)}, u32[]{:S(2)}, u32[]{:S(2)}) collective-permute-start(bf16[1408,128]{1,0:T(8,128)(2,1)} %get-tuple-element.30), channel_id=1, source_target_pairs={{0,2},{1,3},{2,4},{3,5},{4,6},{5,7},{6,0},{7,1},{8,10},{9,11},{10,... | collective-permute-start | bytes 1081352 | tf_op jit(solution)/shard_map/tokens_to_heads/ppermute | solution.py:339
  20.4 1.2 %slots.1 = (bf16[1024,128]{1,0:T(8,128)(2,1)}, bf16[128,512]{1,0:T(8,128)(2,1)S(1)}) custom-call(s32[1]{0:T(128)} %bitcast.seq_ref, bf16[128,640]{1,0:T(8,128)(2,1)S(1)} %bitcast.14, bf16[128,640]{1,0:T(8,128)(2,1)S(1)} %collective-permute-done.near_ref, bf16[128,640]{1,0:T(8,128)(2,1)S(1)} %collective-permute-done.1.far_ref, s32[2,64]{1,0:T(2,128)S(1)} %bitcast.16), custom_call_target="tpu_custom_call" | custom-call | flops 33554432 | bytes 1048576 | tf_op jit(solution)/shard_map/slots/pallas_call | solution.py:36
  21.6 16.6 %all-to-all-start = ((bf16[64,16,128]{2,1,0:T(8,128)(2,1)}), bf16[64,16,128]{2,1,0:T(8,128)(2,1)S(1)}, u32[]{:S(2)}, u32[]{:S(2)}) async-start(bf16[64,16,128]{2,1,0:T(8,128)(2,1)} %bitcast.5), calls=%async_computation | async-start | bytes 524288 | tf_op jit(solution)/shard_map/rows_out/all_to_all | solution.py:375
  38.2 0.0 collective-permute-done.3.refs_2_
  38.2 0.0 collective-permute-done.4.refs_3_
  38.2 0.0 collective-permute-done.2.refs_1_
  38.3 1.9 %collective-permute-start.5 = (bf16[1536,128]{1,0:T(8,128)(2,1)S(1)}, bf16[1536,128]{1,0:T(8,128)(2,1)S(1)}, u32[]{:S(2)}, u32[]{:S(2)}) collective-permute-start(bf16[1536,128]{1,0:T(8,128)(2,1)S(1)} %share_cores.1.mine_ref), channel_id=1, source_target_pairs={{0,1},{1,0},{2,3},{3,2},{4,5},{5,4},{6,7},{7,6},{8,9},{9,8},{10,11... | collective-permute-start | bytes 1179656 | tf_op jit(solution)/shard_map/share_cores/ppermute | solution.py:383
  40.2 11.8 %all-to-all-done = bf16[64,16,128]{2,1,0:T(8,128)(2,1)S(1)} async-done(((bf16[64,16,128]{2,1,0:T(8,128)(2,1)}), bf16[64,16,128]{2,1,0:T(8,128)(2,1)S(1)}, u32[]{:S(2)}, u32[]{:S(2)}) %all-to-all-start) | async-done | bytes 262176 | tf_op jit(solution)/shard_map/rows_out/all_to_all | solution.py:375
  52.0 0.0 collective-permute-done.5.other_ref
  52.0 2.7 %prefix_part.1 = bf16[1152,128]{1,0:T(8,128)(2,1)} custom-call(bf16[1024,128]{1,0:T(8,128)(2,1)S(1)} %bitcast.15, bf16[1536,128]{1,0:T(8,128)(2,1)S(1)} %share_cores.1.mine_ref, bf16[1536,128]{1,0:T(8,128)(2,1)S(1)} %collective-permute-done.5.other_ref), custom_call_target="tpu_custom_call" | custom-call | flops 536870912 | bytes 1048576 | tf_op jit(solution)/shard_map/prefix_part/pallas_call | solution.py:36
  54.7 4.8 %all-to-all-start.1 = ((bf16[64,9,2,128]{3,2,1,0:T(2,128)(2,1)}), bf16[64,9,2,128]{3,2,1,0:T(2,128)(2,1)S(1)}, u32[]{:S(2)}, u32[]{:S(2)}) async-start(bf16[64,9,2,128]{3,2,1,0:T(2,128)(2,1)} %bitcast.7), calls=%async_computation.1 | async-start | bytes 589824 | tf_op jit(solution)/shard_map/rows_back/all_to_all | solution.py:395
  59.5 2.0 %page_part.1 = (f32[136,640]{1,0:T(8,128)S(1)}, f32[136,640]{1,0:T(8,128)S(1)}) custom-call(s32[1]{0:T(128)} %bitcast.seq_ref, bf16[1536,128]{1,0:T(8,128)(2,1)S(1)} %share_cores.1.mine_ref, bf16[1536,128]{1,0:T(8,128)(2,1)S(1)} %collective-permute-done.5.other_ref, s32[2,64]{1,0:T(2,128)S(1)} %copy-done.3, bf16[1536,128]{1,0:T(8,128)(2,1)S(1)} %copy-done.1, ...), custom_call_target="tpu_custom_call" | custom-call | flops 1073741824 | bytes 2097152 | tf_op jit(solution)/shard_map/page_part/pallas_call | solution.py:36
  61.5 1.9 %collective-permute-start.6 = (f32[136,640]{1,0:T(8,128)S(1)}, f32[136,640]{1,0:T(8,128)S(1)}, u32[]{:S(2)}, u32[]{:S(2)}) collective-permute-start(f32[136,640]{1,0:T(8,128)S(1)} %get-tuple-element.34), channel_id=1, source_target_pairs={{0,1},{1,0},{2,3},{3,2},{4,5},{5,4},{6,7},{7,6},{8,9},{9,8},{10,11... | collective-permute-start | bytes 1044488 | tf_op jit(solution)/shard_map/page_part/ppermute | solution.py:405
  63.4 1.6 %collective-permute-done.6.got_ref = f32[136,640]{1,0:T(8,128)S(1)} collective-permute-done((f32[136,640]{1,0:T(8,128)S(1)}, f32[136,640]{1,0:T(8,128)S(1)}, u32[]{:S(2)}, u32[]{:S(2)}) %collective-permute-start.6) | collective-permute-done | bytes 348192 | tf_op jit(solution)/shard_map/page_part/ppermute | solution.py:405
  65.0 0.5 page_merge.1
  65.5 8.0 %all-to-all-done.1 = bf16[64,9,2,128]{3,2,1,0:T(2,128)(2,1)S(1)} async-done(((bf16[64,9,2,128]{3,2,1,0:T(2,128)(2,1)}), bf16[64,9,2,128]{3,2,1,0:T(2,128)(2,1)S(1)}, u32[]{:S(2)}, u32[]{:S(2)}) %all-to-all-start.1) | async-done | bytes 294944 | tf_op jit(solution)/shard_map/rows_back/all_to_all | solution.py:395
  73.5 1.6 %finish.1 = bf16[128,512]{1,0:T(8,128)(2,1)} custom-call(bf16[1152,128]{1,0:T(8,128)(2,1)S(1)} %bitcast.10, f32[128,512]{1,0:T(8,128)S(1)} %get-tuple-element.35.part_ref, f32[128,128]{1,0:T(8,128)S(1)} %get-tuple-element.36.stat_ref, bf16[128,320]{1,0:T(8,128)(2,1)S(1)} %get-tuple-element.37.pick_ref, f32[128,512]{1,0:T(8,128)S(1)} %get-tuple-element.38.mask_ref), custom_call_target="tpu_custom_call" | custom-call | flops 33554432 | bytes 1048576 | tf_op jit(solution)/shard_map/finish/pallas_call | solution.py:36
  (9 shorter events, 0.1 us)
Async XLA Ops:
  0.0 6.8 %collective-permute-start = (bf16[128,640]{1,0:T(8,128)(2,1)}, bf16[128,640]{1,0:T(8,128)(2,1)S(1)}, u32[]{:S(2)}, u32[]{:S(2)}) collective-permute-start(bf16[128,640]{1,0:T(8,128)(2,1)} %bitcast.11), channel_id=1, source_target_pairs={{0,1},{1,2},{2,3},{3,4},{4,5},{5,6},{6,7},{8,9},{9,10},{10,11},{11... | collective-permute-start | bytes 491528 | tf_op jit(solution)/shard_map/rows_to_heads/ppermute | solution.py:342
  1.9 4.9 %collective-permute-start.1 = (bf16[128,640]{1,0:T(8,128)(2,1)}, bf16[128,640]{1,0:T(8,128)(2,1)S(1)}, u32[]{:S(2)}, u32[]{:S(2)}) collective-permute-start(bf16[128,640]{1,0:T(8,128)(2,1)} %bitcast.12), channel_id=1, source_target_pairs={{4,6},{5,7},{12,14},{13,15},{20,22},{21,23},{28,30},{29,31},{36,38... | collective-permute-start | bytes 491528 | tf_op jit(solution)/shard_map/rows_to_heads/ppermute | solution.py:343
  2.6 17.8 %copy-start = (bf16[2,64,640]{2,1,0:T(8,128)(2,1)S(1)}, bf16[2,64,640]{2,1,0:T(8,128)(2,1)}, u32[]{:S(2)}) copy-start(bf16[2,64,640]{2,1,0:T(8,128)(2,1)} %param.5) | copy-start | bytes 491524
  6.8 13.5 %copy-start.2 = (s32[2,64,1]{1,2,0:T(1,128)S(1)}, s32[2,64,1]{1,2,0:T(1,128)}, u32[]{:S(2)}) copy-start(s32[2,64,1]{1,2,0:T(1,128)} %param.6) | copy-start | bytes 1540
  6.8 31.3 %collective-permute-start.3 = (bf16[1408,128]{1,0:T(8,128)(2,1)}, bf16[1408,128]{1,0:T(8,128)(2,1)S(1)}, u32[]{:S(2)}, u32[]{:S(2)}) collective-permute-start(bf16[1408,128]{1,0:T(8,128)(2,1)} %get-tuple-element.31), channel_id=1, source_target_pairs={{0,4},{1,5},{2,6},{3,7},{4,0},{5,1},{6,2},{7,3},{8,12},{9,13},{10,... | collective-permute-start | bytes 1081352 | tf_op jit(solution)/shard_map/tokens_to_heads/ppermute | solution.py:339
  14.5 23.7 %collective-permute-start.4 = (bf16[1408,128]{1,0:T(8,128)(2,1)}, bf16[1408,128]{1,0:T(8,128)(2,1)S(1)}, u32[]{:S(2)}, u32[]{:S(2)}) collective-permute-start(bf16[1408,128]{1,0:T(8,128)(2,1)} %get-tuple-element.32), channel_id=1, source_target_pairs={{0,6},{1,7},{2,0},{3,1},{4,2},{5,3},{6,4},{7,5},{8,14},{9,15},{10,... | collective-permute-start | bytes 1081352 | tf_op jit(solution)/shard_map/tokens_to_heads/ppermute | solution.py:339
  16.7 21.5 %collective-permute-start.2 = (bf16[1408,128]{1,0:T(8,128)(2,1)}, bf16[1408,128]{1,0:T(8,128)(2,1)S(1)}, u32[]{:S(2)}, u32[]{:S(2)}) collective-permute-start(bf16[1408,128]{1,0:T(8,128)(2,1)} %get-tuple-element.30), channel_id=1, source_target_pairs={{0,2},{1,3},{2,4},{3,5},{4,6},{5,7},{6,0},{7,1},{8,10},{9,11},{10,... | collective-permute-start | bytes 1081352 | tf_op jit(solution)/shard_map/tokens_to_heads/ppermute | solution.py:339
  20.4 17.8 %copy-start.1 = (bf16[1536,128]{1,0:T(8,128)(2,1)S(1)}, bf16[1536,128]{1,0:T(8,128)(2,1)}, u32[]{:S(2)}) copy-start(bf16[1536,128]{1,0:T(8,128)(2,1)} %get-tuple-element.29.refs_0_) | copy-start | bytes 1179652
  21.6 30.4 %all-to-all-start = ((bf16[64,16,128]{2,1,0:T(8,128)(2,1)}), bf16[64,16,128]{2,1,0:T(8,128)(2,1)S(1)}, u32[]{:S(2)}, u32[]{:S(2)}) async-start(bf16[64,16,128]{2,1,0:T(8,128)(2,1)} %bitcast.5), calls=%async_computation | async-start | bytes 524288 | tf_op jit(solution)/shard_map/rows_out/all_to_all | solution.py:375
  38.3 13.7 %collective-permute-start.5 = (bf16[1536,128]{1,0:T(8,128)(2,1)S(1)}, bf16[1536,128]{1,0:T(8,128)(2,1)S(1)}, u32[]{:S(2)}, u32[]{:S(2)}) collective-permute-start(bf16[1536,128]{1,0:T(8,128)(2,1)S(1)} %share_cores.1.mine_ref), channel_id=1, source_target_pairs={{0,1},{1,0},{2,3},{3,2},{4,5},{5,4},{6,7},{7,6},{8,9},{9,8},{10,11... | collective-permute-start | bytes 1179656 | tf_op jit(solution)/shard_map/share_cores/ppermute | solution.py:383
  54.7 4.8 %copy-start.3 = (s32[2,64]{1,0:T(2,128)S(1)}, s32[2,64]{1,0:T(2,128)}, u32[]{:S(2)}) copy-start(s32[2,64]{1,0:T(2,128)} %parent_ref.1) | copy-start | bytes 1540
  54.7 18.8 %all-to-all-start.1 = ((bf16[64,9,2,128]{3,2,1,0:T(2,128)(2,1)}), bf16[64,9,2,128]{3,2,1,0:T(2,128)(2,1)S(1)}, u32[]{:S(2)}, u32[]{:S(2)}) async-start(bf16[64,9,2,128]{3,2,1,0:T(2,128)(2,1)} %bitcast.7), calls=%async_computation.1 | async-start | bytes 589824 | tf_op jit(solution)/shard_map/rows_back/all_to_all | solution.py:395
  61.5 3.6 %collective-permute-start.6 = (f32[136,640]{1,0:T(8,128)S(1)}, f32[136,640]{1,0:T(8,128)S(1)}, u32[]{:S(2)}, u32[]{:S(2)}) collective-permute-start(f32[136,640]{1,0:T(8,128)S(1)} %get-tuple-element.34), channel_id=1, source_target_pairs={{0,1},{1,0},{2,3},{3,2},{4,5},{5,4},{6,7},{7,6},{8,9},{9,8},{10,11... | collective-permute-start | bytes 1044488 | tf_op jit(solution)/shard_map/page_part/ppermute | solution.py:405

commit v6 on v4

--- a/solution.py
+++ b/solution.py
@@ -358,8 +358,8 @@
             out="r",
         )
         split = list(split)
-        split[1], near = lax.optimization_barrier((split[1], near))
-        split[2], split[3], far = lax.optimization_barrier((split[2], split[3], far))
+        split[3], near = lax.optimization_barrier((split[3], near))
+        split[2], split[1], far = lax.optimization_barrier((split[2], split[1], far))
         pieces = [split[0]] + [turn(split[k], k) for k in range(1, 4)]
     with jax.named_scope("slots"):
         sent, query = call(

time: 73.9 us -> 74.5 us (level)
  no operation moved by 1% of the time
where the time goes in v6:
time: 74.5 us; the launch traced here: 74 us
  starting transfers between devices  41.2 us (55%)
  waiting for transfers between devices  21.3 us (29%)
  Pallas kernels  10.4 us (14%)
  local copies, waits for them, and re-layouts  0.87 us (1%)
    all_to_all x1, starting transfers between devices, body(): lax.all_to_all(sent, 'prompt', 0, 0, tiled=True).reshape(slots, DH)  16.6 us
    ppermute x3, starting transfers between devices, turn(): lax.ppermute(value, 'seq', [(i, (i + 2 * k) % seq_count) for i in range(s...  13.5 us
    all_to_all x1, waiting for transfers between devices, body(): lax.all_to_all(sent, 'prompt', 0, 0, tiled=True).reshape(slots, DH)  11.5 us
    pallas_call x7, Pallas kernels, call(): pl.pallas_call(kernel, out_shape=(outs,) if single else outs, in_specs=[s...  10.4 us
    all_to_all x1, waiting for transfers between devices, body(): back = lax.all_to_all(part, 'prompt', 0, 0, tiled=True).reshape(-1, DH)  8.16 us
    all_to_all x1, starting transfers between devices, body(): back = lax.all_to_all(part, 'prompt', 0, 0, tiled=True).reshape(-1, DH)  4.75 us
    ppermute x1, starting transfers between devices, body(): got = lax.ppermute(lent, 'seq', swap)  1.92 us
    ppermute x1, starting transfers between devices, body(): other = lax.ppermute(shared, 'seq', swap)  1.92 us
  transfers between devices with their start and end apart: 9, of which 3 were waited for; matrix products, arithmetic and copies ran while one was open for 1% of the time, Pallas kernels for 8%

profile of v6, /device:TPU:2, one launch (start us, length us, event | category | flops | bytes accessed | tf_op | source)
XLA Modules:
  0.0 74.0 jit_solution(1566906359562303006)
XLA Ops:
  0.0 1.9 %collective-permute-start = (bf16[128,640]{1,0:T(8,128)(2,1)}, bf16[128,640]{1,0:T(8,128)(2,1)S(1)}, u32[]{:S(2)}, u32[]{:S(2)}) collective-permute-start(bf16[128,640]{1,0:T(8,128)(2,1)} %bitcast.11), channel_id=1, source_target_pairs={{0,1},{1,2},{2,3},{3,4},{4,5},{5,6},{6,7},{8,9},{9,10},{10,11},{11... | collective-permute-start | bytes 491528 | tf_op jit(solution)/shard_map/rows_to_heads/ppermute | solution.py:342
  1.9 0.8 %slice.4 = bf16[128,256]{1,0:T(8,128)(2,1)S(1)} slice(bf16[128,640]{1,0:T(8,128)(2,1)} %bitcast.12), slice={[0:128], [384:640]} | slice | bytes 131072 | tf_op jit(solution)/shard_map/rows_to_heads/slice | solution.py:343
  2.8 0.7 collective-permute-start.1
  3.4 0.0 copy-start
  3.4 2.5 %tokens_to_heads.1 = (bf16[1536,128]{1,0:T(8,128)(2,1)}, bf16[1408,128]{1,0:T(8,128)(2,1)}, bf16[1408,128]{1,0:T(8,128)(2,1)}, bf16[1408,128]{1,0:T(8,128)(2,1)}) custom-call(s32[1]{0:T(128)} %bitcast.seq_ref, bf16[512,1024]{1,0:T(8,128)(2,1)} %bitcast.18, bf16[128,1024]{1,0:T(8,128)(2,1)} %bitcast.19, bf16[128,640]{1,0:T(8,128)(2,1)} %bitcast.13), custom_call_target="tpu_custom_call" | custom-call | bytes 3145728 | tf_op jit(solution)/shard_map/tokens_to_heads/pallas_call | solution.py:36
  5.9 0.0 collective-permute-done.1.far_ref
  5.9 5.8 %collective-permute-start.2 = (bf16[1408,128]{1,0:T(8,128)(2,1)}, bf16[1408,128]{1,0:T(8,128)(2,1)S(1)}, u32[]{:S(2)}, u32[]{:S(2)}) collective-permute-start(bf16[1408,128]{1,0:T(8,128)(2,1)} %get-tuple-element.30), channel_id=1, source_target_pairs={{0,2},{1,3},{2,4},{3,5},{4,6},{5,7},{6,0},{7,1},{8,10},{9,11},{10,... | collective-permute-start | bytes 1081352 | tf_op jit(solution)/shard_map/tokens_to_heads/ppermute | solution.py:339
  11.8 5.3 %collective-permute-start.3 = (bf16[1408,128]{1,0:T(8,128)(2,1)}, bf16[1408,128]{1,0:T(8,128)(2,1)S(1)}, u32[]{:S(2)}, u32[]{:S(2)}) collective-permute-start(bf16[1408,128]{1,0:T(8,128)(2,1)} %get-tuple-element.31), channel_id=1, source_target_pairs={{0,4},{1,5},{2,6},{3,7},{4,0},{5,1},{6,2},{7,3},{8,12},{9,13},{10,... | collective-permute-start | bytes 1081352 | tf_op jit(solution)/shard_map/tokens_to_heads/ppermute | solution.py:339
  17.1 0.0 copy-start.2
  17.1 2.3 %collective-permute-start.4 = (bf16[1408,128]{1,0:T(8,128)(2,1)}, bf16[1408,128]{1,0:T(8,128)(2,1)S(1)}, u32[]{:S(2)}, u32[]{:S(2)}) collective-permute-start(bf16[1408,128]{1,0:T(8,128)(2,1)} %get-tuple-element.32), channel_id=1, source_target_pairs={{0,6},{1,7},{2,0},{3,1},{4,2},{5,3},{6,4},{7,5},{8,14},{9,15},{10,... | collective-permute-start | bytes 1081352 | tf_op jit(solution)/shard_map/tokens_to_heads/ppermute | solution.py:339
  19.5 1.2 %slots.1 = (bf16[1024,128]{1,0:T(8,128)(2,1)}, bf16[128,512]{1,0:T(8,128)(2,1)S(1)}) custom-call(s32[1]{0:T(128)} %bitcast.seq_ref, bf16[128,640]{1,0:T(8,128)(2,1)S(1)} %bitcast.14, bf16[128,640]{1,0:T(8,128)(2,1)S(1)} %collective-permute-done.near_ref, bf16[128,256]{1,0:T(8,128)(2,1)S(1)} %collective-permute-done.1.far_ref, s32[2,64]{1,0:T(2,128)S(1)} %bitcast.16), custom_call_target="tpu_custom_call" | custom-call | flops 33554432 | bytes 1048576 | tf_op jit(solution)/shard_map/slots/pallas_call | solution.py:36
  20.6 16.6 %all-to-all-start = ((bf16[64,16,128]{2,1,0:T(8,128)(2,1)}), bf16[64,16,128]{2,1,0:T(8,128)(2,1)S(1)}, u32[]{:S(2)}, u32[]{:S(2)}) async-start(bf16[64,16,128]{2,1,0:T(8,128)(2,1)} %bitcast.5), calls=%async_computation | async-start | bytes 524288 | tf_op jit(solution)/shard_map/rows_out/all_to_all | solution.py:375
  37.2 0.0 collective-permute-done.2.refs_1_
  37.3 0.0 collective-permute-done.3.refs_2_
  37.3 1.9 %collective-permute-start.5 = (bf16[1536,128]{1,0:T(8,128)(2,1)S(1)}, bf16[1536,128]{1,0:T(8,128)(2,1)S(1)}, u32[]{:S(2)}, u32[]{:S(2)}) collective-permute-start(bf16[1536,128]{1,0:T(8,128)(2,1)S(1)} %share_cores.1.mine_ref), channel_id=1, source_target_pairs={{0,1},{1,0},{2,3},{3,2},{4,5},{5,4},{6,7},{7,6},{8,9},{9,8},{10,11... | collective-permute-start | bytes 1179656 | tf_op jit(solution)/shard_map/share_cores/ppermute | solution.py:383
  39.3 11.5 %all-to-all-done = bf16[64,16,128]{2,1,0:T(8,128)(2,1)S(1)} async-done(((bf16[64,16,128]{2,1,0:T(8,128)(2,1)}), bf16[64,16,128]{2,1,0:T(8,128)(2,1)S(1)}, u32[]{:S(2)}, u32[]{:S(2)}) %all-to-all-start) | async-done | bytes 262176 | tf_op jit(solution)/shard_map/rows_out/all_to_all | solution.py:375
  50.8 2.7 %prefix_part.1 = bf16[1152,128]{1,0:T(8,128)(2,1)} custom-call(bf16[1024,128]{1,0:T(8,128)(2,1)S(1)} %bitcast.15, bf16[1536,128]{1,0:T(8,128)(2,1)S(1)} %share_cores.1.mine_ref, bf16[1536,128]{1,0:T(8,128)(2,1)S(1)} %collective-permute-done.5.other_ref), custom_call_target="tpu_custom_call" | custom-call | flops 536870912 | bytes 1048576 | tf_op jit(solution)/shard_map/prefix_part/pallas_call | solution.py:36
  53.5 4.8 %all-to-all-start.1 = ((bf16[64,9,2,128]{3,2,1,0:T(2,128)(2,1)}), bf16[64,9,2,128]{3,2,1,0:T(2,128)(2,1)S(1)}, u32[]{:S(2)}, u32[]{:S(2)}) async-start(bf16[64,9,2,128]{3,2,1,0:T(2,128)(2,1)} %bitcast.7), calls=%async_computation.1 | async-start | bytes 589824 | tf_op jit(solution)/shard_map/rows_back/all_to_all | solution.py:395
  58.3 2.0 %page_part.1 = (f32[136,640]{1,0:T(8,128)S(1)}, f32[136,640]{1,0:T(8,128)S(1)}) custom-call(s32[1]{0:T(128)} %bitcast.seq_ref, bf16[1536,128]{1,0:T(8,128)(2,1)S(1)} %share_cores.1.mine_ref, bf16[1536,128]{1,0:T(8,128)(2,1)S(1)} %collective-permute-done.5.other_ref, s32[2,64]{1,0:T(2,128)S(1)} %copy-done.3, bf16[1536,128]{1,0:T(8,128)(2,1)S(1)} %copy-done.1, ...), custom_call_target="tpu_custom_call" | custom-call | flops 1073741824 | bytes 2097152 | tf_op jit(solution)/shard_map/page_part/pallas_call | solution.py:36
  60.3 1.9 %collective-permute-start.6 = (f32[136,640]{1,0:T(8,128)S(1)}, f32[136,640]{1,0:T(8,128)S(1)}, u32[]{:S(2)}, u32[]{:S(2)}) collective-permute-start(f32[136,640]{1,0:T(8,128)S(1)} %get-tuple-element.34), channel_id=1, source_target_pairs={{0,1},{1,0},{2,3},{3,2},{4,5},{5,4},{6,7},{7,6},{8,9},{9,8},{10,11... | collective-permute-start | bytes 1044488 | tf_op jit(solution)/shard_map/page_part/ppermute | solution.py:405
  62.2 1.6 %collective-permute-done.6.got_ref = f32[136,640]{1,0:T(8,128)S(1)} collective-permute-done((f32[136,640]{1,0:T(8,128)S(1)}, f32[136,640]{1,0:T(8,128)S(1)}, u32[]{:S(2)}, u32[]{:S(2)}) %collective-permute-start.6) | collective-permute-done | bytes 348192 | tf_op jit(solution)/shard_map/page_part/ppermute | solution.py:405
  63.8 0.5 page_merge.1
  64.3 8.2 %all-to-all-done.1 = bf16[64,9,2,128]{3,2,1,0:T(2,128)(2,1)S(1)} async-done(((bf16[64,9,2,128]{3,2,1,0:T(2,128)(2,1)}), bf16[64,9,2,128]{3,2,1,0:T(2,128)(2,1)S(1)}, u32[]{:S(2)}, u32[]{:S(2)}) %all-to-all-start.1) | async-done | bytes 294944 | tf_op jit(solution)/shard_map/rows_back/all_to_all | solution.py:395
  72.5 1.6 %finish.1 = bf16[128,512]{1,0:T(8,128)(2,1)} custom-call(bf16[1152,128]{1,0:T(8,128)(2,1)S(1)} %bitcast.10, f32[128,512]{1,0:T(8,128)S(1)} %get-tuple-element.35.part_ref, f32[128,128]{1,0:T(8,128)S(1)} %get-tuple-element.36.stat_ref, bf16[128,320]{1,0:T(8,128)(2,1)S(1)} %get-tuple-element.37.pick_ref, f32[128,512]{1,0:T(8,128)S(1)} %get-tuple-element.38.mask_ref), custom_call_target="tpu_custom_call" | custom-call | flops 33554432 | bytes 1048576 | tf_op jit(solution)/shard_map/finish/pallas_call | solution.py:36
  (10 shorter events, 0.1 us)
Async XLA Ops:
  0.0 17.1 %collective-permute-start = (bf16[128,640]{1,0:T(8,128)(2,1)}, bf16[128,640]{1,0:T(8,128)(2,1)S(1)}, u32[]{:S(2)}, u32[]{:S(2)}) collective-permute-start(bf16[128,640]{1,0:T(8,128)(2,1)} %bitcast.11), channel_id=1, source_target_pairs={{0,1},{1,2},{2,3},{3,4},{4,5},{5,6},{6,7},{8,9},{9,10},{10,11},{11... | collective-permute-start | bytes 491528 | tf_op jit(solution)/shard_map/rows_to_heads/ppermute | solution.py:342
  2.8 3.1 %collective-permute-start.1 = (bf16[128,256]{1,0:T(8,128)(2,1)S(1)}, bf16[128,256]{1,0:T(8,128)(2,1)S(1)}, u32[]{:S(2)}, u32[]{:S(2)}) collective-permute-start(bf16[128,256]{1,0:T(8,128)(2,1)S(1)} %slice.4), channel_id=1, source_target_pairs={{4,6},{5,7},{12,14},{13,15},{20,22},{21,23},{28,30},{29,31},{36,38... | collective-permute-start | bytes 196616 | tf_op jit(solution)/shard_map/rows_to_heads/ppermute | solution.py:343
  3.4 16.0 %copy-start = (bf16[2,64,640]{2,1,0:T(8,128)(2,1)S(1)}, bf16[2,64,640]{2,1,0:T(8,128)(2,1)}, u32[]{:S(2)}) copy-start(bf16[2,64,640]{2,1,0:T(8,128)(2,1)} %param.5) | copy-start | bytes 491524
  5.9 31.3 %collective-permute-start.2 = (bf16[1408,128]{1,0:T(8,128)(2,1)}, bf16[1408,128]{1,0:T(8,128)(2,1)S(1)}, u32[]{:S(2)}, u32[]{:S(2)}) collective-permute-start(bf16[1408,128]{1,0:T(8,128)(2,1)} %get-tuple-element.30), channel_id=1, source_target_pairs={{0,2},{1,3},{2,4},{3,5},{4,6},{5,7},{6,0},{7,1},{8,10},{9,11},{10,... | collective-permute-start | bytes 1081352 | tf_op jit(solution)/shard_map/tokens_to_heads/ppermute | solution.py:339
  11.8 25.5 %collective-permute-start.3 = (bf16[1408,128]{1,0:T(8,128)(2,1)}, bf16[1408,128]{1,0:T(8,128)(2,1)S(1)}, u32[]{:S(2)}, u32[]{:S(2)}) collective-permute-start(bf16[1408,128]{1,0:T(8,128)(2,1)} %get-tuple-element.31), channel_id=1, source_target_pairs={{0,4},{1,5},{2,6},{3,7},{4,0},{5,1},{6,2},{7,3},{8,12},{9,13},{10,... | collective-permute-start | bytes 1081352 | tf_op jit(solution)/shard_map/tokens_to_heads/ppermute | solution.py:339
  17.1 2.3 %copy-start.2 = (s32[2,64,1]{1,2,0:T(1,128)S(1)}, s32[2,64,1]{1,2,0:T(1,128)}, u32[]{:S(2)}) copy-start(s32[2,64,1]{1,2,0:T(1,128)} %param.6) | copy-start | bytes 1540
  17.1 20.1 %collective-permute-start.4 = (bf16[1408,128]{1,0:T(8,128)(2,1)}, bf16[1408,128]{1,0:T(8,128)(2,1)S(1)}, u32[]{:S(2)}, u32[]{:S(2)}) collective-permute-start(bf16[1408,128]{1,0:T(8,128)(2,1)} %get-tuple-element.32), channel_id=1, source_target_pairs={{0,6},{1,7},{2,0},{3,1},{4,2},{5,3},{6,4},{7,5},{8,14},{9,15},{10,... | collective-permute-start | bytes 1081352 | tf_op jit(solution)/shard_map/tokens_to_heads/ppermute | solution.py:339
  19.4 17.8 %copy-start.1 = (bf16[1536,128]{1,0:T(8,128)(2,1)S(1)}, bf16[1536,128]{1,0:T(8,128)(2,1)}, u32[]{:S(2)}) copy-start(bf16[1536,128]{1,0:T(8,128)(2,1)} %get-tuple-element.29.refs_0_) | copy-start | bytes 1179652
  20.6 30.1 %all-to-all-start = ((bf16[64,16,128]{2,1,0:T(8,128)(2,1)}), bf16[64,16,128]{2,1,0:T(8,128)(2,1)S(1)}, u32[]{:S(2)}, u32[]{:S(2)}) async-start(bf16[64,16,128]{2,1,0:T(8,128)(2,1)} %bitcast.5), calls=%async_computation | async-start | bytes 524288 | tf_op jit(solution)/shard_map/rows_out/all_to_all | solution.py:375
  37.3 13.5 %collective-permute-start.5 = (bf16[1536,128]{1,0:T(8,128)(2,1)S(1)}, bf16[1536,128]{1,0:T(8,128)(2,1)S(1)}, u32[]{:S(2)}, u32[]{:S(2)}) collective-permute-start(bf16[1536,128]{1,0:T(8,128)(2,1)S(1)} %share_cores.1.mine_ref), channel_id=1, source_target_pairs={{0,1},{1,0},{2,3},{3,2},{4,5},{5,4},{6,7},{7,6},{8,9},{9,8},{10,11... | collective-permute-start | bytes 1179656 | tf_op jit(solution)/shard_map/share_cores/ppermute | solution.py:383
  53.5 4.8 %copy-start.3 = (s32[2,64]{1,0:T(2,128)S(1)}, s32[2,64]{1,0:T(2,128)}, u32[]{:S(2)}) copy-start(s32[2,64]{1,0:T(2,128)} %parent_ref.1) | copy-start | bytes 1540
  53.5 18.9 %all-to-all-start.1 = ((bf16[64,9,2,128]{3,2,1,0:T(2,128)(2,1)}), bf16[64,9,2,128]{3,2,1,0:T(2,128)(2,1)S(1)}, u32[]{:S(2)}, u32[]{:S(2)}) async-start(bf16[64,9,2,128]{3,2,1,0:T(2,128)(2,1)} %bitcast.7), calls=%async_computation.1 | async-start | bytes 589824 | tf_op jit(solution)/shard_map/rows_back/all_to_all | solution.py:395
  60.3 3.6 %collective-permute-start.6 = (f32[136,640]{1,0:T(8,128)S(1)}, f32[136,640]{1,0:T(8,128)S(1)}, u32[]{:S(2)}, u32[]{:S(2)}) collective-permute-start(f32[136,640]{1,0:T(8,128)S(1)} %get-tuple-element.34), channel_id=1, source_target_pairs={{0,1},{1,0},{2,3},{3,2},{4,5},{5,4},{6,7},{7,6},{8,9},{9,8},{10,11... | collective-permute-start | bytes 1044488 | tf_op jit(solution)/shard_map/page_part/ppermute | solution.py:405
